TPU v7x, 512 devices: a whole 4x4x16 slice. The times are simulated.
512 devices in a mesh: orb: 8 (over y, x_lo), grid: 64 (over x_hi, z, core).
Axes of the slice: x: 4 (x_hi: 2, x_lo: 2; x = x_hi * 2 + x_lo), y: 4, z: 16, core: 2. Of those that a mesh axis runs over, the one named last changes fastest.
Arguments:
- random_orbitals: float32 [8, 256, 256, 256], P('orb', 'grid'), may hold values from -6 to 6
- potential: float32 [256, 256, 256], P('grid'), may hold values from -1.5 to 0.5
- sphere_cells: int32 [1024, 2, 128], P('grid'), may hold values from 0 to 65535, as said below
- projectors: float32 [1024, 4, 128], P('grid'), may hold values from -0.9 to 0.9
- kb_energy: float32 [4], replicated, may hold values from 0.5 to 1.5
- cheb_coef: float32 [3], replicated, may hold values from 0.5 to 1.5
Outputs:
- density: float32 [256, 256, 256], P('grid')
Inputs may be any that keep to these rules, and one draw needn't show every extreme that they name: `sphere_cells`: for each atom a the 128 points are distinct cells: the 128 offsets (dz, dy, dx) with |dz|, |dy|, |dx| <= 3 nearest to the atom's centre, ties broken by the order of (dz, dy, dx) from smallest to largest, added to the centre with periodic wrap along each dimension; row 0 holds the z-plane and row 1 the cell y * 256 + x. The centre's z lies in the slab of planes (a // 16) * 4 to (a // 16) * 4 + 3. Spheres of different atoms may share cells.
All inputs are finite; a program needn't handle non-finite values.
Results may differ from a plain program's by a relative error of at most 0.0002.
Values sent between devices are 32-bit elements; how exact they have to be, the bound alone decides.
A program may use at most 64 MiB of HBM per device.

v0:
```python
import math

import jax
import jax.numpy as jnp
from jax import lax
from jax.sharding import PartitionSpec as P

REACH = 3


PRECISE = lax.Precision.HIGHEST
CENTRE = 2.0
HALF_RANGE = 4.0


def with_halo(cells, sides, width):
    for axis, dim in sides:
        count = lax.axis_size(axis)
        head = lax.slice_in_dim(cells, 0, width, axis=dim)
        tail = lax.slice_in_dim(cells, cells.shape[dim] - width, cells.shape[dim], axis=dim)
        cells = jnp.concatenate(
            [
                lax.ppermute(tail, axis, [(i, (i + 1) % count) for i in range(count)]),
                cells,
                lax.ppermute(head, axis, [((i + 1) % count, i) for i in range(count)]),
            ],
            axis=dim,
        )
    return cells


def from_behind(block, axis, distance):
    devices = range(lax.axis_size(axis))
    route = [((i - distance) % len(devices), i) for i in devices]
    return lax.ppermute(block, axis, route)


def kinetic_table(length):
    places = jnp.arange(length)
    offset = places[:, None] - places[None, :]
    parity = jnp.where(offset % 2 == 0, 1.0, -1.0).astype(jnp.float32)
    angle_half = offset.astype(jnp.float32) * (math.pi / length)
    sine = jnp.where(offset == 0, 1.0, jnp.sin(angle_half))
    off_diag = parity / (2.0 * sine * sine)
    on_diag = jnp.float32(length * length / 12.0 + 1.0 / 6.0)
    return jnp.where(offset == 0, on_diag, off_diag) * (4.0 / (length * length))


def local(random_orbitals, potential, sphere_cells, projectors, kb_energy, cheb_coef):
    grid_count = lax.axis_size("grid")
    grid_pos = lax.axis_index("grid")
    planes = potential.shape[0]
    rows_y = potential.shape[1]
    cols_x = potential.shape[2]
    all_planes = planes * grid_count
    plane_cells = rows_y * cols_x
    first_plane = grid_pos * planes
    orb_count = random_orbitals.shape[0]
    per_dev = sphere_cells.shape[0]
    kinetic_x = kinetic_table(cols_x)
    kinetic_y = kinetic_table(rows_y)
    kinetic_z = kinetic_table(all_planes)

    def along_z(columns):
        turned = jnp.einsum("ozyx,zw->owyx", columns, kinetic_z, precision=PRECISE)
        return lax.all_to_all(turned, "grid", split_axis=1, concat_axis=2, tiled=True)

    z_glob = sphere_cells[:, 0, :]
    in_plane = sphere_cells[:, 1, :]
    local_plane = (z_glob - first_plane + REACH) % all_planes
    ghost_index = (local_plane * plane_cells + in_plane).reshape(-1)

    def nonlocal_term(vector):
        extended = with_halo(vector, (("grid", 1),), REACH)
        flattened = extended.reshape(orb_count, -1)
        values = flattened[:, ghost_index].reshape(orb_count, per_dev, -1)
        coeffs = jnp.einsum("oaj,apj->oap", values, projectors, precision=PRECISE) * kb_energy
        spread = jnp.einsum("oap,apj->oaj", coeffs, projectors, precision=PRECISE).reshape(
            orb_count, -1
        )
        placed = jnp.zeros_like(flattened).at[:, ghost_index].add(spread).reshape(extended.shape)
        lower_rim = placed[:, :REACH]
        upper_rim = placed[:, REACH + planes :]
        from_above = from_behind(lower_rim, "grid", -1)
        from_below = from_behind(upper_rim, "grid", 1)
        interior = placed[:, REACH : REACH + planes]
        interior = interior.at[:, :REACH].add(from_below)
        interior = interior.at[:, planes - REACH :].add(from_above)
        return interior

    def apply_hamiltonian(vector):
        kinetic = jnp.dot(vector.reshape(-1, cols_x), kinetic_x, precision=PRECISE).reshape(
            vector.shape
        )
        kinetic = kinetic + jnp.einsum("ozyx,yw->ozwx", vector, kinetic_y, precision=PRECISE)
        kinetic = kinetic + along_z(
            lax.all_to_all(vector, "grid", split_axis=2, concat_axis=1, tiled=True)
        )
        summed = kinetic + potential * vector + nonlocal_term(vector)
        return (summed - CENTRE * vector) / HALF_RANGE

    first_term = apply_hamiltonian(random_orbitals)
    second_term = 2.0 * apply_hamiltonian(first_term) - random_orbitals
    filtered = (
        cheb_coef[0] * random_orbitals + cheb_coef[1] * first_term + cheb_coef[2] * second_term
    )
    group_density = jnp.sum(filtered * filtered, axis=0)
    density = lax.psum(group_density, "orb")
    return density / (orb_count * lax.axis_size("orb"))


def solution(mesh):
    in_specs = (
        P("orb", "grid", None, None),
        P("grid", None, None),
        P("grid", None, None),
        P("grid", None, None),
        P(),
        P(),
    )
    out_specs = P("grid", None, None)
    return jax.shard_map(local, mesh=mesh, in_specs=in_specs, out_specs=out_specs, check_vma=False)
```

profile of v0, /device:TPU:1, one launch (start us, length us, event | category | flops | bytes accessed | tf_op | source)
XLA Modules:
  0.0 503.8 jit_solution(14557212406994386126)
XLA Ops:
  6.5 1.9 copy.20
  8.4 71.3 %all_to_all.66 = f32[1,4,256,256]{3,1,0,2:T(4,128)S(1)} all-to-all(f32[1,4,256,256]{3,1,0,2:T(4,128)S(1)} %copy.20), channel_id=1, replica_groups=mesh['orb'=8,'grid'=64] {'grid'}, dimensions={2} | all-to-all | bytes 2097152 | tf_op jit(solution)/shard_map/all_to_all | solution.py:97
  80.3 2.1 convolution_bitcast_fusion.3
  82.4 1.6 copy.22
  84.0 10.0 %all-to-all-start.1 = ((f32[1,256,4,256]{3,2,0,1:T(4,128)}), f32[1,256,4,256]{3,2,0,1:T(4,128)}, u32[]{:S(2)}, u32[]{:S(2)}) async-start(f32[1,256,4,256]{3,2,0,1:T(4,128)} %copy.22), calls=%async_computation.1 | async-start | bytes 2097152 | tf_op jit(solution)/shard_map/all_to_all | solution.py:66
  94.0 1.0 fusion.111
  95.0 3.5 collective-permute-start
  98.6 1.9 collective-permute-start.1
  100.6 47.1 %collective-permute-done = f32[1,3,256,256]{3,2,1,0:T(8,128)S(1)} collective-permute-done((f32[1,3,256,256]{3,2,1,0:T(8,128)}, f32[1,3,256,256]{3,2,1,0:T(8,128)S(1)}, u32[]{:S(2)}, u32[]{:S(2)}) %collective-permute-start) | collective-permute-done | bytes 786464 | tf_op jit(solution)/shard_map/ppermute | solution.py:23
  147.6 2.1 collective-permute-done.1
  149.9 1.3 copy.40
  151.2 11.8 %gather_fusion = f32[2048]{0:T(1024)S(1)} fusion(f32[655360]{0:T(1024)S(1)} %bitcast.161, s32[2048]{0:T(1024)S(1)} %broadcast_clamp_fusion), kind=kCustom, calls=%fused_computation | custom fusion | bytes 24576 | tf_op jit(solution)/shard_map/gather | solution.py:76
  163.6 12.0 %scatter_custom_fusion = f32[655360]{0:T(1024)S(1)} fusion(s32[2048]{0:T(1024)S(1)} %bitcast.173, f32[2048]{0:T(1024)S(1)} %bitcast.182, f32[]{:T(128)} %constant.158.clone.1), kind=kCustom, calls=%fused_computation.14 | custom fusion | flops 2048 | bytes 2621444 | tf_op jit(solution)/shard_map/scatter-add | solution.py:81
  175.6 1.9 reshape.291
  177.5 2.8 fusion.109
  180.3 2.2 collective-permute-start.2
  182.5 6.0 %collective-permute-start.3 = (f32[1,3,256,256]{3,2,1,0:T(8,128)}, f32[1,3,256,256]{3,2,1,0:T(8,128)}, u32[]{:S(2)}, u32[]{:S(2)}) collective-permute-start(f32[1,3,256,256]{3,2,1,0:T(8,128)} %get-tuple-element.55), channel_id=1, source_target_pairs={{1,0},{2,1},{3,2},{4,3},{5,4},{6,5},{7,6},{8,7},{9,8},{10,9},{11,1... | collective-permute-start | bytes 2359304 | tf_op jit(solution)/shard_map/ppermute | solution.py:35
  188.6 2.1 convolution_bitcast_fusion.5
  190.7 1.3 copy.38
  192.0 1.5 fusion.26
  193.5 3.0 collective-permute-done.3
  196.5 1.3 fusion.25
  197.8 1.4 copy.48
  199.2 1.3 all_to_all.54
  200.5 5.2 %broadcast_multiply_fusion.1 = (f32[1,4,256,256]{3,2,1,0:T(8,128)S(1)}, f32[1,4,256,256]{3,2,1,0:T(8,128)}) fusion(f32[1,4,256,256]{3,2,1,0:T(8,128)S(1)} %copy-done.2, f32[1,4,256,256]{3,2,1,0:T(8,128)S(1)} %fusion.25, f32[4,256,256]{2,1,0:T(8,128)} %param.15, f32[1,4,256,256]{3,2,1,0:T(8,128)} %all_to_all.54, f32[1,4,256,256]{3,2,1,0:T(8,128)} %bitcast.165), kind=kOutput, calls=%fused_computation.50 | convolution fusion | flops 808910848 | bytes 7340032 | tf_op jit(solution)/shard_map/ozyx,yw->ozwx/dot_general | solution.py:95
  206.4 66.5 %all_to_all.67 = f32[1,4,256,256]{3,1,0,2:T(4,128)S(1)} all-to-all(f32[1,4,256,256]{3,1,0,2:T(4,128)S(1)} %copy.25), channel_id=1, replica_groups=mesh['orb'=8,'grid'=64] {'grid'}, dimensions={2} | all-to-all | bytes 2097152 | tf_op jit(solution)/shard_map/all_to_all | solution.py:97
  273.4 2.1 convolution_bitcast_fusion
  275.5 1.7 copy.27
  277.2 9.8 %all-to-all-start.3 = ((f32[1,256,4,256]{3,2,0,1:T(4,128)}), f32[1,256,4,256]{3,2,0,1:T(4,128)}, u32[]{:S(2)}, u32[]{:S(2)}) async-start(f32[1,256,4,256]{3,2,0,1:T(4,128)} %copy.27), calls=%async_computation.3 | async-start | bytes 2097152 | tf_op jit(solution)/shard_map/all_to_all | solution.py:66
  287.2 3.5 collective-permute-start.4
  290.7 2.1 collective-permute-start.5
  292.9 47.6 %collective-permute-done.4 = f32[1,3,256,256]{3,2,1,0:T(8,128)S(1)} collective-permute-done((f32[1,3,256,256]{3,2,1,0:T(8,128)S(1)}, f32[1,3,256,256]{3,2,1,0:T(8,128)S(1)}, u32[]{:S(2)}, u32[]{:S(2)}) %collective-permute-start.4) | collective-permute-done | bytes 786464 | tf_op jit(solution)/shard_map/ppermute | solution.py:23
  340.5 2.2 collective-permute-done.5
  342.9 1.3 copy.41
  344.3 11.8 %gather_fusion.1 = f32[2048]{0:T(1024)S(1)} fusion(f32[655360]{0:T(1024)S(1)} %bitcast.160, s32[2048]{0:T(1024)S(1)} %broadcast_clamp_fusion), kind=kCustom, calls=%fused_computation.1 | custom fusion | bytes 24576 | tf_op jit(solution)/shard_map/gather | solution.py:76
  356.6 13.0 %scatter_custom_fusion.1 = f32[655360]{0:T(1024)} fusion(s32[2048]{0:T(1024)S(1)} %bitcast.174, f32[2048]{0:T(1024)S(1)} %bitcast.181, f32[]{:T(128)} %constant.158.clone.1), kind=kCustom, calls=%fused_computation.12 | custom fusion | flops 2048 | bytes 2621444 | tf_op jit(solution)/shard_map/scatter-add | solution.py:81
  369.6 2.7 reshape.296
  372.6 2.3 collective-permute-start.6
  374.9 5.8 %collective-permute-start.7 = (f32[1,3,256,256]{3,2,1,0:T(8,128)S(1)}, f32[1,3,256,256]{3,2,1,0:T(8,128)S(1)}, u32[]{:S(2)}, u32[]{:S(2)}) collective-permute-start(f32[1,3,256,256]{3,2,1,0:T(8,128)S(1)} %get-tuple-element.53), channel_id=1, source_target_pairs={{1,0},{2,1},{3,2},{4,3},{5,4},{6,5},{7,6},{8,7},{9,8},{10,9},{11,1... | collective-permute-start | bytes 2359304 | tf_op jit(solution)/shard_map/ppermute | solution.py:35
  382.0 3.1 convolution_bitcast_fusion.1
  385.1 1.1 slice.193
  387.2 1.3 collective-permute-done.7
  388.5 2.2 fusion.23
  390.7 2.5 copy.46
  393.2 2.6 all_to_all.61
  395.8 6.6 %fusion.21 = f32[4,256,256]{2,1,0:T(8,128)} fusion(f32[1,4,256,256]{3,2,1,0:T(8,128)S(1)} %copy-done.3, f32[1,4,256,256]{3,2,1,0:T(8,128)} %fusion.23, f32[4,256,256]{2,1,0:T(8,128)S(1)} %copy-done.4, f32[1,4,256,256]{3,2,1,0:T(8,128)S(1)} %copy-done.6, f32[]{:T(128)} %bitcast.28, f32[]{:T(128)} %bitcast.27, f32[]{:T(128)} %bitcast, ...), kind=kOutput, calls=%fused_computation.35 | convolution fusion | flops 811270144 | bytes 7340044 | tf_op jit(solution)/shard_map/dot_general | solution.py:92
  402.4 92.3 %all-reduce.2.cloned.1.call-done = f32[4,256,256]{2,1,0:T(8,128)} async-done(((f32[4,256,256]{2,1,0:T(8,128)}), f32[4,256,256]{2,1,0:T(8,128)}) %all-reduce.2.cloned.1.call-update) | async-done | bytes 1048592 | tf_op jit(solution)/shard_map/psum | solution.py:108
  494.6 2.3 broadcast_multiply_fusion
  (47 shorter events, 5.3 us)
Async XLA Ops:
  6.5 156.5 %copy-start = (f32[16,4,128]{2,1,0:T(4,128)S(1)}, f32[16,4,128]{2,1,0:T(4,128)}, u32[]{:S(2)}) copy-start(f32[16,4,128]{2,1,0:T(4,128)} %param.17) | copy-start | bytes 98308
  82.3 11.6 %copy-start.1 = (f32[1,4,256,256]{3,2,1,0:T(8,128)S(1)}, f32[1,4,256,256]{3,2,1,0:T(8,128)}, u32[]{:S(2)}) copy-start(f32[1,4,256,256]{3,2,1,0:T(8,128)} %param.14) | copy-start | bytes 3145732
  84.0 16.5 %copy-start.7 = (s32[16,2,128]{2,1,0:T(2,128)S(1)}, s32[16,2,128]{2,1,0:T(2,128)}, u32[]{:S(2)}) copy-start(s32[16,2,128]{2,1,0:T(2,128)} %param.16) | copy-start | bytes 49156
  84.0 113.8 %all-to-all-start.1 = ((f32[1,256,4,256]{3,2,0,1:T(4,128)}), f32[1,256,4,256]{3,2,0,1:T(4,128)}, u32[]{:S(2)}, u32[]{:S(2)}) async-start(f32[1,256,4,256]{3,2,0,1:T(4,128)} %copy.22), calls=%async_computation.1 | async-start | bytes 2097152 | tf_op jit(solution)/shard_map/all_to_all | solution.py:66
  95.0 52.6 %collective-permute-start = (f32[1,3,256,256]{3,2,1,0:T(8,128)}, f32[1,3,256,256]{3,2,1,0:T(8,128)S(1)}, u32[]{:S(2)}, u32[]{:S(2)}) collective-permute-start(f32[1,3,256,256]{3,2,1,0:T(8,128)} %get-tuple-element.59), channel_id=1, source_target_pairs={{0,1},{1,2},{2,3},{3,4},{4,5},{5,6},{6,7},{7,8},{8,9},{9,10},{10,1... | collective-permute-start | bytes 2359304 | tf_op jit(solution)/shard_map/ppermute | solution.py:23
  98.6 51.1 %collective-permute-start.1 = (f32[1,3,256,256]{3,2,1,0:T(8,128)S(1)}, f32[1,3,256,256]{3,2,1,0:T(8,128)S(1)}, u32[]{:S(2)}, u32[]{:S(2)}) collective-permute-start(f32[1,3,256,256]{3,2,1,0:T(8,128)S(1)} %get-tuple-element.60), channel_id=1, source_target_pairs={{1,0},{2,1},{3,2},{4,3},{5,4},{6,5},{7,6},{8,7},{9,8},{10,9},{11,1... | collective-permute-start | bytes 2359304 | tf_op jit(solution)/shard_map/ppermute | solution.py:25
  151.2 12.1 %copy-start.9 = (f32[4]{0:T(128)S(1)}, f32[4]{0:T(128)}, u32[]{:S(2)}) copy-start(f32[4]{0:T(128)} %param.18) | copy-start | bytes 52
  177.5 11.1 %copy-start.2 = (f32[1,4,256,256]{3,2,1,0:T(8,128)S(1)}, f32[1,4,256,256]{3,2,1,0:T(8,128)}, u32[]{:S(2)}) copy-start(f32[1,4,256,256]{3,2,1,0:T(8,128)} %param.14) | copy-start | bytes 3145732
  180.3 11.7 %collective-permute-start.2 = (f32[1,3,256,256]{3,2,1,0:T(8,128)}, f32[1,3,256,256]{3,2,1,0:T(8,128)}, u32[]{:S(2)}, u32[]{:S(2)}) collective-permute-start(f32[1,3,256,256]{3,2,1,0:T(8,128)} %get-tuple-element.56), channel_id=1, source_target_pairs={{63,0},{0,1},{1,2},{2,3},{3,4},{4,5},{5,6},{6,7},{7,8},{8,9},{9,10... | collective-permute-start | bytes 2359304 | tf_op jit(solution)/shard_map/ppermute | solution.py:35
  182.5 13.9 %collective-permute-start.3 = (f32[1,3,256,256]{3,2,1,0:T(8,128)}, f32[1,3,256,256]{3,2,1,0:T(8,128)}, u32[]{:S(2)}, u32[]{:S(2)}) collective-permute-start(f32[1,3,256,256]{3,2,1,0:T(8,128)} %get-tuple-element.55), channel_id=1, source_target_pairs={{1,0},{2,1},{3,2},{4,3},{5,4},{6,5},{7,6},{8,7},{9,8},{10,9},{11,1... | collective-permute-start | bytes 2359304 | tf_op jit(solution)/shard_map/ppermute | solution.py:35
  190.7 1.3 slice-start
  277.2 113.5 %all-to-all-start.3 = ((f32[1,256,4,256]{3,2,0,1:T(4,128)}), f32[1,256,4,256]{3,2,0,1:T(4,128)}, u32[]{:S(2)}, u32[]{:S(2)}) async-start(f32[1,256,4,256]{3,2,0,1:T(4,128)} %copy.27), calls=%async_computation.3 | async-start | bytes 2097152 | tf_op jit(solution)/shard_map/all_to_all | solution.py:66
  287.0 207.7 %all-reduce.2.cloned.1.call-start = ((), (), s32[]{:S(2)}) async-start(), calls=%async_computation.4 | async-start | bytes 2097152 | tf_op jit(solution)/shard_map/psum | solution.py:108
  287.2 53.3 %collective-permute-start.4 = (f32[1,3,256,256]{3,2,1,0:T(8,128)S(1)}, f32[1,3,256,256]{3,2,1,0:T(8,128)S(1)}, u32[]{:S(2)}, u32[]{:S(2)}) collective-permute-start(f32[1,3,256,256]{3,2,1,0:T(8,128)S(1)} %get-tuple-element.57), channel_id=1, source_target_pairs={{0,1},{1,2},{2,3},{3,4},{4,5},{5,6},{6,7},{7,8},{8,9},{9,10},{10,1... | collective-permute-start | bytes 2359304 | tf_op jit(solution)/shard_map/ppermute | solution.py:23
  290.7 52.0 %collective-permute-start.5 = (f32[1,3,256,256]{3,2,1,0:T(8,128)S(1)}, f32[1,3,256,256]{3,2,1,0:T(8,128)S(1)}, u32[]{:S(2)}, u32[]{:S(2)}) collective-permute-start(f32[1,3,256,256]{3,2,1,0:T(8,128)S(1)} %get-tuple-element.58), channel_id=1, source_target_pairs={{1,0},{2,1},{3,2},{4,3},{5,4},{6,5},{7,6},{8,7},{9,8},{10,9},{11,1... | collective-permute-start | bytes 2359304 | tf_op jit(solution)/shard_map/ppermute | solution.py:25
  372.4 8.4 %copy-start.8 = (f32[3]{0:T(128)S(1)}, f32[3]{0:T(128)}, u32[]{:S(2)}) copy-start(f32[3]{0:T(128)} %param.19) | copy-start | bytes 40
  372.4 9.7 %copy-start.5 = (f32[1,4,256,256]{3,2,1,0:T(8,128)S(1)}, f32[1,4,256,256]{3,2,1,0:T(8,128)}, u32[]{:S(2)}) copy-start(f32[1,4,256,256]{3,2,1,0:T(8,128)} %get-tuple-element.65) | copy-start | bytes 3145732
  372.6 13.6 %collective-permute-start.6 = (f32[1,3,256,256]{3,2,1,0:T(8,128)S(1)}, f32[1,3,256,256]{3,2,1,0:T(8,128)S(1)}, u32[]{:S(2)}, u32[]{:S(2)}) collective-permute-start(f32[1,3,256,256]{3,2,1,0:T(8,128)S(1)} %get-tuple-element.54), channel_id=1, source_target_pairs={{63,0},{0,1},{1,2},{2,3},{3,4},{4,5},{5,6},{6,7},{7,8},{8,9},{9,10... | collective-permute-start | bytes 2359304 | tf_op jit(solution)/shard_map/ppermute | solution.py:35
  374.9 13.6 %collective-permute-start.7 = (f32[1,3,256,256]{3,2,1,0:T(8,128)S(1)}, f32[1,3,256,256]{3,2,1,0:T(8,128)S(1)}, u32[]{:S(2)}, u32[]{:S(2)}) collective-permute-start(f32[1,3,256,256]{3,2,1,0:T(8,128)S(1)} %get-tuple-element.53), channel_id=1, source_target_pairs={{1,0},{2,1},{3,2},{4,3},{5,4},{6,5},{7,6},{8,7},{9,8},{10,9},{11,1... | collective-permute-start | bytes 2359304 | tf_op jit(solution)/shard_map/ppermute | solution.py:35
  390.7 5.1 %copy-start.3 = (f32[1,4,256,256]{3,2,1,0:T(8,128)S(1)}, f32[1,4,256,256]{3,2,1,0:T(8,128)}, u32[]{:S(2)}) copy-start(f32[1,4,256,256]{3,2,1,0:T(8,128)} %param.14) | copy-start | bytes 3145732
  390.7 5.1 %copy-start.4 = (f32[4,256,256]{2,1,0:T(8,128)S(1)}, f32[4,256,256]{2,1,0:T(8,128)}, u32[]{:S(2)}) copy-start(f32[4,256,256]{2,1,0:T(8,128)} %param.15) | copy-start | bytes 3145732
  390.7 5.1 %copy-start.6 = (f32[1,4,256,256]{3,2,1,0:T(8,128)S(1)}, f32[1,4,256,256]{3,2,1,0:T(8,128)}, u32[]{:S(2)}) copy-start(f32[1,4,256,256]{3,2,1,0:T(8,128)} %get-tuple-element.65) | copy-start | bytes 3145732
Sparse Core Ops, SparseCore 0:
  402.5 92.0 all-reduce.1
where the time goes:
time: 508 us; the launch traced here: 504 us
  waiting for transfers between devices  195 us (38%)
  blocking collectives  138 us (27%)
  local copies, waits for them, and re-layouts  52.9 us (10%)
  starting transfers between devices  47.4 us (9%)
  other arithmetic  33.7 us (7%)
  matrix products  22.1 us (4%)
  between operations  14.4 us (3%)
    all_to_all x2, blocking collectives, apply_hamiltonian(): lax.all_to_all(vector, 'grid', split_axis=2, concat_axis=1, tiled=True)  138 us
    ppermute x2, waiting for transfers between devices, with_halo(): lax.ppermute(tail, axis, [(i, (i + 1) % count) for i in range(count)])  94.7 us
    psum x1, waiting for transfers between devices, local(): density = lax.psum(group_density, 'orb')  92.3 us
    scatter-add x2, other arithmetic, nonlocal_term(): jnp.zeros_like(flattened).at[:, ghost_index].add(spread)  25.1 us
    gather x2, local copies, waits for them, and re-layouts, nonlocal_term(): values = flattened[:, ghost_index].reshape(orb_count, per_dev, -1)  23.6 us
    all_to_all x2, starting transfers between devices, along_z(): lax.all_to_all(turned, 'grid', split_axis=1, concat_axis=2, tiled=True)  19.8 us
    ppermute x4, starting transfers between devices, from_behind(): return lax.ppermute(block, axis, route)  16.4 us
  transfers between devices with their start and end apart: 11, of which 7 were waited for; matrix products, arithmetic and copies ran while one was open for 15% of the time, Pallas kernels for 0%

commit v1 on v0

v1 whole, which is shorter than its diff:
```python
import functools

import jax
import jax.numpy as jnp
import numpy as np
from jax import lax
from jax.experimental import pallas as pl
from jax.experimental.pallas import tpu as pltpu
from jax.sharding import Mesh, PartitionSpec as P

AXES = ("y", "xl", "xh", "zb", "par", "core")
SIZES = {"y": 4, "xl": 2, "xh": 2, "zb": 8, "par": 2, "core": 2}
PLANE = ("y", "xl", "xh")
LINE = ("zb", "par", "core")
BLOCK = ("y", "xl", "xh", "par")
QUAD = ("y", "xl", "xh", "par", "core")

N = 256
REACH = 3
SPH = 128
HIGH = lax.Precision.HIGH
MESH = pl.DeviceIdType.MESH
F32 = jnp.float32


def kinetic_table(length):
    places = np.arange(length)
    offset = places[:, None] - places[None, :]
    parity = np.where(offset % 2 == 0, 1.0, -1.0)
    sine = np.where(offset == 0, 1.0, np.sin(offset * (np.pi / length)))
    table = np.where(offset == 0, length * length / 12.0 + 1.0 / 6.0, parity / (2.0 * sine * sine))
    return (table * (4.0 / (length * length))).astype(np.float32)


def sphere_offsets():
    width = 2 * REACH + 1
    count = width**3
    ids = np.arange(count)
    off = np.stack([ids // (width * width), ids // width % width, ids % width], axis=1) - REACH
    radius = (off * off).sum(axis=1)
    return off[np.argsort(radius * count + ids, kind="stable")[:SPH]]


def cube_places():
    off = sphere_offsets() + REACH
    table = np.zeros((SPH, 512), np.float32)
    table[np.arange(SPH), off[:, 1] * 64 + off[:, 0] * 8 + off[:, 2]] = 1.0
    return table


def index_of(axes):
    where = 0
    for name in axes:
        where = where * SIZES[name] + lax.axis_index(name)
    return where


def coords_of(axes, where):
    coords = {}
    for name in reversed(axes):
        coords[name] = lax.rem(where, SIZES[name])
        where = where // SIZES[name]
    return coords


def group_size(axes):
    return int(np.prod([SIZES[name] for name in axes]))


def greet_group(axes):
    me, count = index_of(axes), group_size(axes)
    barrier = pltpu.get_barrier_semaphore()

    def greet(k, carry):
        pl.semaphore_signal(
            barrier, inc=1, device_id=coords_of(axes, lax.rem(me + k, count)), device_id_type=MESH
        )
        return carry

    lax.fori_loop(1, count, greet, 0)
    return barrier, count - 1


def swap_start(axes, source, target, send, recv):
    me, count = index_of(axes), group_size(axes)

    def step(k, carry):
        peer = lax.rem(me + k, count)
        pltpu.make_async_remote_copy(
            src_ref=source(peer),
            dst_ref=target(me),
            send_sem=send.at[peer],
            recv_sem=recv.at[me],
            device_id=coords_of(axes, peer),
            device_id_type=MESH,
        ).start()
        return carry

    lax.fori_loop(1, count, step, 0)
    pltpu.make_async_copy(source(me), target(me), recv.at[me]).start()


def swap_wait(axes, source, target, send, recv):
    me, count = index_of(axes), group_size(axes)

    def step(k, carry):
        peer = lax.rem(me + k, count)
        copy = pltpu.make_async_remote_copy(
            src_ref=source(peer),
            dst_ref=target(peer),
            send_sem=send.at[peer],
            recv_sem=recv.at[peer],
            device_id=coords_of(axes, peer),
            device_id_type=MESH,
        )
        copy.wait_send()
        copy.wait_recv()
        return carry

    lax.fori_loop(1, count, step, 0)
    pltpu.make_async_copy(source(me), target(me), recv.at[me]).wait()


def comm_call(kernel, cid, outs, scratch, *operands):
    return pl.pallas_call(
        kernel,
        out_shape=[jax.ShapeDtypeStruct(shape, F32) for shape in outs],
        in_specs=[pl.BlockSpec(memory_space=pl.ANY)] * len(operands),
        out_specs=[pl.BlockSpec(memory_space=pl.ANY)] * len(outs),
        scratch_shapes=scratch,
        compiler_params=pltpu.CompilerParams(collective_id=cid, has_side_effects=True),
    )(*operands)


def dma(*shape):
    return pltpu.SemaphoreType.DMA(shape)


def spread_rows(v_ref, pot_ref, v_out, pot_out, send, recv, psend, precv):
    xh = lax.axis_index("xh")
    me = index_of(PLANE)
    barrier, greeted = greet_group(PLANE)
    pl.semaphore_wait(barrier, greeted)

    def source(peer):
        return v_ref.at[:, pl.ds(pl.multiple_of(peer * 16, 16), 16), :]

    def target(peer):
        return v_out.at[peer]

    swap_start(PLANE, source, target, send, recv)
    other = me + 1 - 2 * xh
    pot_copy = pltpu.make_async_remote_copy(
        src_ref=pot_ref.at[:, pl.ds(pl.multiple_of(other * 16, 16), 16), :],
        dst_ref=pot_out.at[xh],
        send_sem=psend.at[0],
        recv_sem=precv.at[xh],
        device_id={"xh": 1 - xh},
        device_id_type=MESH,
    )
    pot_copy.start()
    own = pltpu.make_async_copy(
        pot_ref.at[:, pl.ds(pl.multiple_of(me * 16, 16), 16), :], pot_out.at[xh], precv.at[xh]
    )
    own.start()
    swap_wait(PLANE, source, target, send, recv)
    pot_copy.wait_send()
    pltpu.make_async_remote_copy(
        src_ref=pot_ref.at[:, pl.ds(pl.multiple_of(other * 16, 16), 16), :],
        dst_ref=pot_out.at[1 - xh],
        send_sem=psend.at[0],
        recv_sem=precv.at[1 - xh],
        device_id={"xh": 1 - xh},
        device_id_type=MESH,
    ).wait_recv()
    own.wait()


def spread_planes(v_ref, pot_ref, v_out, pot_out, send, recv, psend, precv):
    barrier, greeted = greet_group(LINE)
    pl.semaphore_wait(barrier, greeted)

    def cut(peer):
        rows = pl.ds(pl.multiple_of(lax.rem(peer // 2, 2) * 8, 8), 8)
        cols = pl.ds(pl.multiple_of(lax.rem(peer, 2) * 128, 128), 128)
        return rows, cols

    def source(peer):
        rows, cols = cut(peer)
        return v_ref.at[peer // 4, :, :, rows, cols]

    def target(peer):
        return v_out.at[:, peer]

    def pot_source(peer):
        rows, cols = cut(peer)
        return pot_ref.at[:, :, rows, cols]

    def pot_target(peer):
        return pot_out.at[:, peer]

    swap_start(LINE, source, target, send, recv)
    swap_start(LINE, pot_source, pot_target, psend, precv)
    swap_wait(LINE, source, target, send, recv)
    swap_wait(LINE, pot_source, pot_target, psend, precv)


def home_of(orbital, slab):
    return {
        "y": orbital // 2,
        "xl": lax.rem(orbital, 2),
        "xh": slab // 32,
        "zb": lax.rem(slab // 4, 8),
        "par": lax.rem(slab // 2, 2),
        "core": lax.rem(slab, 2),
    }


def full(coords):
    return tuple(coords[name] for name in AXES)


def is_me(coords):
    same = coords["y"] == lax.axis_index("y")
    for name in AXES[1:]:
        same = jnp.logical_and(same, coords[name] == lax.axis_index(name))
    return same


def spread_atoms(at_ref, at_out, send, recv):
    slab = index_of(("xh", "zb", "par", "core"))
    orbital = index_of(("y", "xl"))
    odd = lax.rem(slab, 2)
    chip, near = slab // 2, lax.rem(slab // 2 + 2 * odd - 1 + 32, 32)
    barrier = pltpu.get_barrier_semaphore()
    mine, zb = index_of(BLOCK), lax.axis_index("zb")
    own = jnp.int32(0)
    homes = [home_of(zb, lax.rem(2 * mine - 1 + slot + 64, 64)) for slot in range(4)]
    sends = []
    for n, (q, slot) in enumerate(((chip, 1 + odd), (near, 3 - 3 * odd))):
        for core in range(2):
            place = coords_of(BLOCK, q)
            place["zb"] = orbital
            place["core"] = jnp.int32(core)
            sends.append((place, slot, 2 * n + core))
    for home in homes:
        same = is_me(home)
        own = own + same.astype(jnp.int32)

        @pl.when(jnp.logical_not(same))
        def _():
            pl.semaphore_signal(barrier, inc=1, device_id=full(home), device_id_type=MESH)

    pl.semaphore_wait(barrier, 4 - own)

    def each(go):
        for place, slot, n in sends:
            same = is_me(place)

            @pl.when(jnp.logical_not(same))
            def _():
                copy = pltpu.make_async_remote_copy(
                    src_ref=at_ref,
                    dst_ref=at_out.at[slot],
                    send_sem=send.at[n],
                    recv_sem=recv.at[slot],
                    device_id=full(place),
                    device_id_type=MESH,
                )
                if go:
                    copy.start()
                else:
                    copy.wait_send()

            @pl.when(same)
            def _():
                copy = pltpu.make_async_copy(at_ref, at_out.at[slot], send.at[n])
                if go:
                    copy.start()
                else:
                    copy.wait()

    each(True)
    each(False)
    for slot, home in enumerate(homes):
        @pl.when(jnp.logical_not(is_me(home)))
        def _():
            pltpu.make_async_remote_copy(
                src_ref=at_ref,
                dst_ref=at_out.at[slot],
                send_sem=send.at[0],
                recv_sem=recv.at[slot],
                device_id=full(home),
                device_id_type=MESH,
            ).wait_recv()


def to_planes(y_ref, z_out, sib_out, send, recv, ssend, srecv):
    core = lax.axis_index("core")
    barrier, greeted = greet_group(BLOCK)
    pl.semaphore_signal(barrier, inc=1, device_id={"core": 1 - core}, device_id_type=MESH)
    pl.semaphore_wait(barrier, greeted + 1)

    def source(peer):
        return y_ref.at[peer]

    def target(peer):
        return z_out.at[:, pl.ds(pl.multiple_of(peer * 8, 8), 8), :]

    swap_start(BLOCK, source, target, send, recv)
    copy = pltpu.make_async_remote_copy(
        src_ref=y_ref,
        dst_ref=sib_out,
        send_sem=ssend.at[0],
        recv_sem=srecv.at[0],
        device_id={"core": 1 - core},
        device_id_type=MESH,
    )
    copy.start()
    swap_wait(BLOCK, source, target, send, recv)
    copy.wait()


def to_rows(z_ref, y_out, send, recv):
    barrier, greeted = greet_group(BLOCK)
    pl.semaphore_wait(barrier, greeted)

    def source(peer):
        return z_ref.at[:, pl.ds(pl.multiple_of(peer * 8, 8), 8), :]

    def target(peer):
        return y_out.at[peer]

    swap_start(BLOCK, source, target, send, recv)
    swap_wait(BLOCK, source, target, send, recv)


def share_coeffs(c_ref, c_out, send, recv):
    core, me = lax.axis_index("core"), index_of(BLOCK)
    up, down = lax.rem(me + 1, 32), lax.rem(me + 31, 32)

    def place(chip, which):
        coords = coords_of(BLOCK, chip)
        coords["core"] = which
        return coords

    peers = [(place(me, 1 - core), jnp.int32(0), 0)]
    for n in range(2):
        which = lax.rem(core + n, 2)
        peers.append((place(up, which), 1 + core, 1 + which))
        peers.append((place(down, which), 3 + core, 3 + which))
    barrier = pltpu.get_barrier_semaphore()
    for coords, _, _ in peers:
        pl.semaphore_signal(barrier, inc=1, device_id=coords, device_id_type=MESH)
    pl.semaphore_wait(barrier, 5)
    copies = []
    for n, (coords, slot, _) in enumerate(peers):
        copies.append(
            pltpu.make_async_remote_copy(
                src_ref=c_ref,
                dst_ref=c_out.at[slot],
                send_sem=send.at[n],
                recv_sem=recv.at[slot],
                device_id=coords,
                device_id_type=MESH,
            )
        )
        copies[-1].start()
    for copy in copies:
        copy.wait_send()
    for slot in range(5):
        pltpu.make_async_remote_copy(
            src_ref=c_ref,
            dst_ref=c_out.at[slot],
            send_sem=send.at[0],
            recv_sem=recv.at[slot],
            device_id=peers[0][0],
            device_id_type=MESH,
        ).wait_recv()


def gather_squares(f_ref, parts_out, send, recv):
    axes = ("zb",)
    barrier, greeted = greet_group(axes)
    pl.semaphore_wait(barrier, greeted)

    def source(peer):
        return f_ref.at[:, peer]

    def target(peer):
        return parts_out.at[peer]

    swap_start(axes, source, target, send, recv)
    swap_wait(axes, source, target, send, recv)


def place_density(s_ref, out_ref, send, recv):
    barrier, greeted = greet_group(QUAD)
    pl.semaphore_wait(barrier, greeted)

    def source(peer):
        return s_ref.at[lax.rem(peer // 4, 2), lax.rem(peer // 2, 2), lax.rem(peer, 2)]

    def target(peer):
        rows = pl.ds(pl.multiple_of(peer // 2 * 8, 8), 8)
        cols = pl.ds(pl.multiple_of(lax.rem(peer, 2) * 128, 128), 128)
        return out_ref.at[:, rows, cols]

    swap_start(QUAD, source, target, send, recv)
    swap_wait(QUAD, source, target, send, recv)


def local(random_orbitals, potential, sphere_cells, projectors, kb_energy, cheb_coef):
    table = kinetic_table(N)
    chip = index_of(BLOCK)
    core = lax.axis_index("core")

    v_rows, pot_rows = comm_call(
        spread_rows, 1, [(16, 4, 16, N), (2, 4, 16, N)], [dma(16), dma(16), dma(1), dma(2)],
        random_orbitals[0], potential,
    )
    v, pot = comm_call(
        spread_planes, 2, [(2, 32, 4, 8, 128)] * 2, [dma(32)] * 4,
        v_rows.reshape(8, 2, 4, 16, N), pot_rows,
    )
    v, pot = v.reshape(N, 8, 128), pot.reshape(N, 8, 128)

    lanes = lax.broadcasted_iota(jnp.int32, (16, 128), 1)
    centres = sphere_cells[:, :, 0].astype(F32)
    marks = jnp.where(lanes == 0, centres[:, 0:1], jnp.where(lanes == 1, centres[:, 1:2], 0.0))
    packed = jnp.concatenate([projectors.reshape(64, SPH), marks], axis=0)
    (atoms,) = comm_call(spread_atoms, 3, [(4, 80, 128)], [dma(4), dma(4)], packed)
    proj = atoms[:, :64].reshape(64, 4, SPH)
    centre_z = atoms[:, 64:, 0].reshape(64).astype(jnp.int32)
    cell = atoms[:, 64:, 1].reshape(64).astype(jnp.int32)
    centre_y, centre_x = cell // N, cell % N

    steps = jnp.arange(8, dtype=jnp.int32) - REACH
    rows_hit = jnp.arange(N)[None, None, :] == ((centre_y[:, None] + steps) % N)[:, :, None]
    pick_rows = rows_hit.astype(F32).reshape(512, N)
    planes_hit = (
        8 * chip + jnp.arange(8)[None, None, :] == ((centre_z[:, None] + steps) % N)[:, :, None]
    ).astype(F32)
    cols_hit = (
        128 * core + jnp.arange(128)[None, None, :] == ((centre_x[:, None] + steps) % N)[:, :, None]
    ).astype(F32)
    cube = jnp.dot(proj.reshape(256, SPH), cube_places(), precision=lax.Precision.HIGHEST)
    cube = cube.reshape(64, 4, 8, 8, 8)
    cube = jnp.einsum("apydx,adz->apyzx", cube, planes_hit, precision=lax.Precision.HIGHEST)
    frames = jnp.einsum("apyzx,axw->apyzw", cube, cols_hit, precision=lax.Precision.HIGHEST)

    def nonlocal_term(planes):
        picked = jnp.einsum("cy,zyx->czx", pick_rows, planes, precision=HIGH).reshape(64, 1, 8, 8, 128)
        part = jnp.sum(frames * picked, axis=(2, 3, 4))
        part = jnp.pad(part.reshape(2, 128), ((0, 6), (0, 0)))
        (others,) = comm_call(share_coeffs, 4, [(5, 8, 128)], [dma(5), dma(5)], part)
        low = part[0] + others[0, 0] + others[1, 1] + others[2, 1]
        high = part[1] + others[0, 1] + others[3, 0] + others[4, 0]
        coeffs = jnp.concatenate([low, high]).reshape(64, 4) * kb_energy
        spread = jnp.sum(coeffs[:, :, None, None, None] * frames, axis=1).reshape(512, 8, 128)
        return jnp.einsum("cy,czx->zyx", pick_rows, spread, precision=HIGH)

    def apply_shifted(rows):
        planes, sibling = comm_call(
            to_planes, 5, [(8, N, 128), (32, 8, 8, 128)], [dma(32), dma(32), dma(1), dma(1)],
            rows.reshape(32, 8, 8, 128),
        )
        in_rows = jnp.einsum("wz,zrx->wrx", table, rows, precision=HIGH)
        in_rows = in_rows + jnp.dot(rows, table[:128, :128], precision=HIGH)
        in_rows = in_rows + jnp.dot(sibling.reshape(N, 8, 128), table[128:, :128], precision=HIGH)
        in_rows = in_rows + (pot - 2.0) * rows
        in_planes = jnp.einsum("wy,zyx->zwx", table, planes, precision=HIGH) + nonlocal_term(planes)
        (back,) = comm_call(to_rows, 6, [(32, 8, 8, 128)], [dma(32), dma(32)], in_planes)
        return (back.reshape(N, 8, 128) + in_rows) / 4.0

    first = apply_shifted(v)
    second = 2.0 * apply_shifted(first) - v
    filtered = cheb_coef[0] * v + cheb_coef[1] * first + cheb_coef[2] * second
    squares = (filtered * filtered).reshape(2, 8, 16, 8, 128)
    (parts,) = comm_call(gather_squares, 7, [(8, 2, 16, 8, 128)], [dma(8), dma(8)], squares)
    summed = (jnp.sum(parts, axis=0) / 8.0).reshape(2, 2, 2, 4, 8, 128)
    (density,) = comm_call(place_density, 8, [(4, N, N)], [dma(64), dma(64)], summed)
    return density


def solution(mesh):
    apart = Mesh(mesh.devices.reshape([SIZES[name] for name in AXES]), AXES)
    orb, grid = ("y", "xl"), ("xh", "zb", "par", "core")
    in_specs = (P(orb, grid), P(grid), P(grid), P(grid), P(), P())
    return jax.shard_map(local, mesh=apart, in_specs=in_specs, out_specs=P(grid), check_vma=False)
```

time: 508 us -> 446 us (0.88)
  Pallas kernels: 0 us -> 350 us
  waiting for transfers between devices: 195 us -> 0 us
  blocking collectives: 138 us -> 0 us
  starting transfers between devices: 47.4 us -> 0 us
  local copies, waits for them, and re-layouts: 52.9 us -> 28.4 us
  matrix products: 22.1 us -> 44.3 us
  between operations: 14.4 us -> 1.07 us
  other arithmetic: 33.7 us -> 20.6 us
    pallas_call x0 -> x11, Pallas kernels: none -> 350 us  [comm_call(): pl.pallas_call(kernel, out_shape=[jax.ShapeDtypeStruct(shape, F32) for sh...]
    all_to_all x2 -> x0, blocking collectives: 138 us -> none  [apply_hamiltonian(): lax.all_to_all(vector, 'grid', split_axis=2, concat_axis=1, tiled=True)]
    ppermute x8 -> x0, waiting for transfers between devices: 103 us -> none  [the longest x2 94.7 us: with_halo(): lax.ppermute(tail, axis, [(i, (i + 1) % count) for i in range(count)])]
    psum x1 -> x0, waiting for transfers between devices: 92.3 us -> none  [local(): density = lax.psum(group_density, 'orb')]
    scatter-add x6 -> x0, other arithmetic: 31 us -> none  [the longest x2 25.1 us: nonlocal_term(): jnp.zeros_like(flattened).at[:, ghost_index].add(spread)]
    ppermute x8 -> x0, starting transfers between devices: 27.6 us -> none  [the longest x4 16.4 us: from_behind(): return lax.ppermute(block, axis, route)]
    gather x2 -> x0, local copies, waits for them, and re-layouts: 23.6 us -> none  [nonlocal_term(): values = flattened[:, ghost_index].reshape(orb_count, per_dev, -1)]
    dot_general x10 -> x15, matrix products: 22.1 us -> 44.3 us  [the longest x1 10.6 us: local(): jnp.einsum('apydx,adz->apyzx', cube, planes_hit, precision=lax.Precision....]
  transfers between devices with their start and end apart: 11 -> 0, of which waited for: 7 -> 0; matrix products, arithmetic and copies ran while one was open for 15% -> 0% of each run, Pallas kernels for 0% -> 0%
where the time goes in v1:
time: 446 us; the launch traced here: 445 us
  Pallas kernels  350 us (78%)
  matrix products  44.3 us (10%)
  local copies, waits for them, and re-layouts  28.4 us (6%)
  other arithmetic  20.6 us (5%)
    pallas_call x11, Pallas kernels, comm_call(): pl.pallas_call(kernel, out_shape=[jax.ShapeDtypeStruct(shape, F32) for sh...  350 us
    dot_general x1, matrix products, local(): jnp.einsum('apydx,adz->apyzx', cube, planes_hit, precision=lax.Precision....  10.6 us
    dot_general x1, matrix products, local(): jnp.einsum('apyzx,axw->apyzw', cube, cols_hit, precision=lax.Precision.HI...  9.76 us
    reduce_sum x2, other arithmetic, nonlocal_term(): jnp.sum(coeffs[:, :, None, None, None] * frames, axis=1)  9.21 us

profile of v1, /device:TPU:1, one launch (start us, length us, event | category | flops | bytes accessed | tf_op | source)
XLA Modules:
  0.0 444.5 jit_solution(15471410037498137167)
XLA Ops:
  0.0 0.8 copy.163
  0.9 1.4 pad_maximum_fusion.at_ref
  2.3 38.8 %shard_map.148 = f32[4,80,128]{2,1,0:T(8,128)} custom-call(f32[80,128]{1,0:T(8,128)} %pad_maximum_fusion.at_ref), custom_call_target="tpu_custom_call" | custom-call | tf_op jit(solution)/shard_map/pallas_call | solution.py:125
  41.1 1.1 convert_reduce_fusion
  42.6 0.9 slice.88
  43.5 2.0 fusion.48
  45.5 7.4 %copy.109 = f32[64,4,8,8,8]{4,3,2,1,0:T(8,128)} copy(f32[64,4,8,8,8]{0,4,3,2,1:T(8,128)S(1)} %fusion.48) | data formatting | bytes 1048576 | tf_op jit(solution)/shard_map/dot_general | solution.py:447
  52.9 10.6 %fusion.44 = f32[64,8,4,8,8]{4,1,3,2,0:T(8,128)} fusion(f32[64,4,8,8,8]{4,3,2,1,0:T(8,128)} %copy.109, s32[64,8]{1,0:T(8,128)S(1)} %copy.107, s32[8]{0:T(128)S(1)} %iota_add_fusion.2), kind=kOutput, calls=%fused_computation.49 | convolution fusion | flops 12587008 | bytes 1050656 | tf_op jit(solution)/shard_map/apydx,adz->apyzx/dot_general | solution.py:449
  63.4 17.9 %shard_map.145 = (f32[16,4,16,256]{3,2,1,0:T(8,128)}, f32[2,4,16,256]{3,2,1,0:T(8,128)}) custom-call(f32[4,256,256]{2,1,0:T(8,128)} %bitcast.97, f32[4,256,256]{2,1,0:T(8,128)} %pot_ref.1), custom_call_target="tpu_custom_call" | custom-call | tf_op jit(solution)/shard_map/pallas_call | solution.py:125
  81.3 108.5 %shard_map.146 = (f32[2,32,4,8,128]{4,3,2,1,0:T(8,128)}, f32[2,32,4,8,128]{4,3,2,1,0:T(8,128)}) custom-call(f32[8,2,4,16,256]{4,3,2,1,0:T(8,128)} %bitcast.96, f32[2,4,16,256]{3,2,1,0:T(8,128)} %get-tuple-element.14.pot_ref), custom_call_target="tpu_custom_call" | custom-call | tf_op jit(solution)/shard_map/pallas_call | solution.py:125
  189.8 20.8 %shard_map.147 = (f32[8,256,128]{2,1,0:T(8,128)}, f32[32,8,8,128]{3,2,1,0:T(8,128)}) custom-call(f32[32,8,8,128]{3,2,1,0:T(8,128)} %bitcast.84), custom_call_target="tpu_custom_call" | custom-call | tf_op jit(solution)/shard_map/pallas_call | solution.py:125
  210.7 2.0 fusion.25
  212.7 1.2 copy.112
  214.0 9.8 %multiply_reduce_fusion.3 = (f32[64,4]{1,0:T(8,128)S(1)}, f32[64,4,8,8,128]{4,3,2,1,0:T(8,128)}) fusion(f32[64,8,8,128]{3,2,1,0:T(8,128)S(1)} %copy.112, s32[64,8]{1,0:T(8,128)S(1)} %copy.110, s32[128]{0:T(128)S(1)} %iota_add_fusion, f32[64,8,4,8,8]{4,1,3,2,0:T(8,128)} %fusion.44), kind=kOutput, calls=%fused_computation.5 | convolution fusion | flops 205586176 | bytes 11013632 | tf_op jit(solution)/shard_map/apyzx,axw->apyzw/dot_general | solution.py:450
  224.5 9.3 %shard_map.149 = f32[5,8,128]{2,1,0:T(8,128)} custom-call(f32[8,128]{1,0:T(8,128)} %pad.7.c_ref), custom_call_target="tpu_custom_call" | custom-call | tf_op jit(solution)/shard_map/pallas_call | solution.py:125
  233.8 0.8 slice_reduce_fusion.11
  235.6 4.6 %multiply_reduce_fusion.2 = f32[64,8,8,128]{3,2,1,0:T(8,128)S(1)} fusion(f32[64,4,8,8,128]{4,3,2,1,0:T(8,128)} %get-tuple-element.50, f32[64,4]{1,0:T(8,128)S(1)} %copy.115), kind=kLoop, calls=%fused_computation.4 | loop fusion | flops 3670016 | bytes 10486784 | tf_op jit(solution)/shard_map/reduce_sum | solution.py:460
  240.2 1.9 fusion.6
  242.1 1.6 fusion.20.z_ref
  243.7 21.5 %shard_map.150 = f32[32,8,8,128]{3,2,1,0:T(8,128)} custom-call(f32[8,256,128]{2,1,0:T(8,128)} %fusion.20.z_ref), custom_call_target="tpu_custom_call" | custom-call | tf_op jit(solution)/shard_map/pallas_call | solution.py:125
  265.2 0.7 fusion.30
  266.0 1.5 convolution_add_fusion.3
  267.6 2.4 broadcast_multiply_fusion
  270.0 1.6 copy.125
  271.6 20.1 %shard_map.151 = (f32[8,256,128]{2,1,0:T(8,128)}, f32[32,8,8,128]{3,2,1,0:T(8,128)}) custom-call(f32[32,8,8,128]{3,2,1,0:T(8,128)} %bitcast.92), custom_call_target="tpu_custom_call" | custom-call | tf_op jit(solution)/shard_map/pallas_call | solution.py:125
  291.7 2.0 fusion.23
  293.8 1.2 copy.128
  295.0 4.5 %multiply_reduce_fusion.1 = f32[64,4]{1,0:T(8,128)S(1)} fusion(f32[64,4,8,8,128]{4,3,2,1,0:T(8,128)} %get-tuple-element.50, f32[64,8,8,128]{3,2,1,0:T(8,128)S(1)} %copy.128), kind=kLoop, calls=%fused_computation.3 | loop fusion | flops 4194048 | bytes 10486784 | tf_op jit(solution)/shard_map/reduce_sum | solution.py:454
  300.2 11.1 %shard_map.152 = f32[5,8,128]{2,1,0:T(8,128)} custom-call(f32[8,128]{1,0:T(8,128)} %pad.8.c_ref), custom_call_target="tpu_custom_call" | custom-call | tf_op jit(solution)/shard_map/pallas_call | solution.py:125
  311.2 1.3 slice_reduce_fusion.5
  312.7 0.8 squeeze.61
  313.4 1.4 squeeze.62
  315.5 0.7 squeeze.64
  316.9 1.4 fusion.57
  318.3 0.8 copy.129
  319.1 0.8 copy.130
  319.9 0.7 maximum_multiply_fusion.1
  320.7 4.6 %multiply_reduce_fusion = f32[64,8,8,128]{3,2,1,0:T(8,128)S(1)} fusion(f32[64,4,8,8,128]{4,3,2,1,0:T(8,128)} %get-tuple-element.50, f32[64,4]{1,0:T(8,128)S(1)} %copy.131), kind=kLoop, calls=%fused_computation.2 | loop fusion | flops 3670016 | bytes 10486784 | tf_op jit(solution)/shard_map/reduce_sum | solution.py:460
  325.4 1.9 fusion.9
  327.3 1.6 fusion.19.z_ref
  328.9 21.1 %shard_map.153 = f32[32,8,8,128]{3,2,1,0:T(8,128)} custom-call(f32[8,256,128]{2,1,0:T(8,128)} %fusion.19.z_ref), custom_call_target="tpu_custom_call" | custom-call | tf_op jit(solution)/shard_map/pallas_call | solution.py:125
  350.6 1.4 convolution_add_fusion.1
  353.4 4.3 fusion.22
  357.7 1.6 copy.139
  359.3 56.5 %shard_map.154 = f32[8,2,16,8,128]{4,3,2,1,0:T(8,128)} custom-call(f32[2,8,16,8,128]{4,3,2,1,0:T(8,128)} %bitcast.93), custom_call_target="tpu_custom_call" | custom-call | tf_op jit(solution)/shard_map/pallas_call | solution.py:125
  415.7 1.3 reduce_sum.49
  417.7 24.5 %shard_map.155 = f32[4,256,256]{2,1,0:T(8,128)} custom-call(f32[2,2,2,4,8,128]{5,4,3,2,1,0:T(8,128)} %bitcast.99), custom_call_target="tpu_custom_call" | custom-call | tf_op jit(solution)/shard_map/pallas_call | solution.py:125
  442.2 2.3 copy.191
  (54 shorter events, 6.6 us)
Async XLA Ops:
  214.0 21.4 %copy-start.8 = (f32[4]{0:T(128)S(1)}, f32[4]{0:T(128)}, u32[]{:S(2)}) copy-start(f32[4]{0:T(128)} %param.19) | copy-start | bytes 52
  223.8 18.4 %copy-start.2 = (f32[8,256,128]{2,1,0:T(8,128)S(1)}, f32[8,256,128]{2,1,0:T(8,128)}, u32[]{:S(2)}) copy-start(f32[8,256,128]{2,1,0:T(8,128)} %get-tuple-element.16) | copy-start | bytes 3145732
  223.8 18.4 %copy-start.4 = (f32[256,256,1]{1,0,2:T(8,128)S(1)}, f32[256,256,1]{1,0,2:T(8,128)}, u32[]{:S(2)}) copy-start(f32[256,256,1]{1,0,2:T(8,128)} %constant.116) | copy-start | bytes 786436
  235.6 29.7 %copy-start = (f32[2,32,4,8,128]{4,3,2,1,0:T(8,128)S(1)}, f32[2,32,4,8,128]{4,3,2,1,0:T(8,128)}, u32[]{:S(2)}) copy-start(f32[2,32,4,8,128]{4,3,2,1,0:T(8,128)} %get-tuple-element.15) | copy-start | bytes 3145732
  240.2 27.3 %copy-start.5 = (f32[2,32,4,8,128]{4,3,2,1,0:T(8,128)S(1)}, f32[2,32,4,8,128]{4,3,2,1,0:T(8,128)}, u32[]{:S(2)}) copy-start(f32[2,32,4,8,128]{4,3,2,1,0:T(8,128)} %get-tuple-element.18) | copy-start | bytes 3145732
  240.2 27.4 %copy-start.6 = (f32[128,128,1]{1,0,2:T(8,128)S(1)}, f32[128,128,1]{1,0,2:T(8,128)}, u32[]{:S(2)}) copy-start(f32[128,128,1]{1,0,2:T(8,128)} %constant.119) | copy-start | bytes 196612
  265.2 2.4 copy-start.1
  320.7 6.6 %copy-start.3 = (f32[8,256,128]{2,1,0:T(8,128)S(1)}, f32[8,256,128]{2,1,0:T(8,128)}, u32[]{:S(2)}) copy-start(f32[8,256,128]{2,1,0:T(8,128)} %get-tuple-element.19) | copy-start | bytes 3145732
  325.3 26.7 %copy-start.7 = (f32[3]{0:T(128)S(1)}, f32[3]{0:T(128)}, u32[]{:S(2)}) copy-start(f32[3]{0:T(128)} %param.20) | copy-start | bytes 40

commit v2 on v1

--- a/solution.py
+++ b/solution.py
@@ -18,7 +18,6 @@
 N = 256
 REACH = 3
 SPH = 128
-HIGH = lax.Precision.HIGH
 MESH = pl.DeviceIdType.MESH
 F32 = jnp.float32
 
@@ -39,13 +38,6 @@
     off = np.stack([ids // (width * width), ids // width % width, ids % width], axis=1) - REACH
     radius = (off * off).sum(axis=1)
     return off[np.argsort(radius * count + ids, kind="stable")[:SPH]]
-
-
-def cube_places():
-    off = sphere_offsets() + REACH
-    table = np.zeros((SPH, 512), np.float32)
-    table[np.arange(SPH), off[:, 1] * 64 + off[:, 0] * 8 + off[:, 2]] = 1.0
-    return table
 
 
 def index_of(axes):
@@ -295,90 +287,6 @@
             ).wait_recv()
 
 
-def to_planes(y_ref, z_out, sib_out, send, recv, ssend, srecv):
-    core = lax.axis_index("core")
-    barrier, greeted = greet_group(BLOCK)
-    pl.semaphore_signal(barrier, inc=1, device_id={"core": 1 - core}, device_id_type=MESH)
-    pl.semaphore_wait(barrier, greeted + 1)
-
-    def source(peer):
-        return y_ref.at[peer]
-
-    def target(peer):
-        return z_out.at[:, pl.ds(pl.multiple_of(peer * 8, 8), 8), :]
-
-    swap_start(BLOCK, source, target, send, recv)
-    copy = pltpu.make_async_remote_copy(
-        src_ref=y_ref,
-        dst_ref=sib_out,
-        send_sem=ssend.at[0],
-        recv_sem=srecv.at[0],
-        device_id={"core": 1 - core},
-        device_id_type=MESH,
-    )
-    copy.start()
-    swap_wait(BLOCK, source, target, send, recv)
-    copy.wait()
-
-
-def to_rows(z_ref, y_out, send, recv):
-    barrier, greeted = greet_group(BLOCK)
-    pl.semaphore_wait(barrier, greeted)
-
-    def source(peer):
-        return z_ref.at[:, pl.ds(pl.multiple_of(peer * 8, 8), 8), :]
-
-    def target(peer):
-        return y_out.at[peer]
-
-    swap_start(BLOCK, source, target, send, recv)
-    swap_wait(BLOCK, source, target, send, recv)
-
-
-def share_coeffs(c_ref, c_out, send, recv):
-    core, me = lax.axis_index("core"), index_of(BLOCK)
-    up, down = lax.rem(me + 1, 32), lax.rem(me + 31, 32)
-
-    def place(chip, which):
-        coords = coords_of(BLOCK, chip)
-        coords["core"] = which
-        return coords
-
-    peers = [(place(me, 1 - core), jnp.int32(0), 0)]
-    for n in range(2):
-        which = lax.rem(core + n, 2)
-        peers.append((place(up, which), 1 + core, 1 + which))
-        peers.append((place(down, which), 3 + core, 3 + which))
-    barrier = pltpu.get_barrier_semaphore()
-    for coords, _, _ in peers:
-        pl.semaphore_signal(barrier, inc=1, device_id=coords, device_id_type=MESH)
-    pl.semaphore_wait(barrier, 5)
-    copies = []
-    for n, (coords, slot, _) in enumerate(peers):
-        copies.append(
-            pltpu.make_async_remote_copy(
-                src_ref=c_ref,
-                dst_ref=c_out.at[slot],
-                send_sem=send.at[n],
-                recv_sem=recv.at[slot],
-                device_id=coords,
-                device_id_type=MESH,
-            )
-        )
-        copies[-1].start()
-    for copy in copies:
-        copy.wait_send()
-    for slot in range(5):
-        pltpu.make_async_remote_copy(
-            src_ref=c_ref,
-            dst_ref=c_out.at[slot],
-            send_sem=send.at[0],
-            recv_sem=recv.at[slot],
-            device_id=peers[0][0],
-            device_id_type=MESH,
-        ).wait_recv()
-
-
 def gather_squares(f_ref, parts_out, send, recv):
     axes = ("zb",)
     barrier, greeted = greet_group(axes)
@@ -410,11 +318,337 @@
     swap_wait(QUAD, source, target, send, recv)
 
 
+def split3(table):
+    high = table.astype(jnp.bfloat16)
+    low = (table - high.astype(np.float32)).astype(jnp.bfloat16)
+    return high, low
+
+
+def split(x):
+    high = x.astype(jnp.bfloat16)
+    return high, (x - high.astype(F32)).astype(jnp.bfloat16)
+
+
+def mm(a, b):
+    return lax.dot_general(a, b, (((1,), (0,)), ((), ())), preferred_element_type=F32)
+
+
+def mm_nt(a, b):
+    return lax.dot_general(a, b, (((1,), (1,)), ((), ())), preferred_element_type=F32)
+
+
+def wrapped(x):
+    x = jnp.where(x < 0.0, x + 256.0, x)
+    return jnp.where(x > 255.0, x - 256.0, x)
+
+
+def along_z(x_ref, out_ref, kl_ref):
+    table = kl_ref[...]
+    for pair in range(4):
+        x = jnp.concatenate([x_ref[:, 2 * pair, :], x_ref[:, 2 * pair + 1, :]], axis=1)
+        high, low = split(x)
+        res = mm(table, jnp.concatenate([high, low, high], axis=0))
+        out_ref[:, 2 * pair, :] = res[:, :128]
+        out_ref[:, 2 * pair + 1, :] = res[:, 128:]
+
+
+def along_x(x_ref, sib_ref, pot_ref, out_ref, kr_ref):
+    def step(n, carry):
+        zs = pl.ds(n * 32, 32)
+        x = x_ref[zs]
+        both = jnp.concatenate([x.reshape(256, 128), sib_ref[zs].reshape(256, 128)], axis=1)
+        high, low = split(both)
+        res = mm(jnp.concatenate([high, low, high], axis=1), kr_ref[...])
+        out_ref[zs] += res.reshape(32, 8, 128) + (pot_ref[zs] - 2.0) * x
+        return carry
+
+    lax.fori_loop(0, 8, step, 0)
+
+
+def two_planes(z_ref, n):
+    return split(jnp.concatenate([z_ref[2 * n], z_ref[2 * n + 1]], axis=1))
+
+
+def along_y(z_ref, out_ref, kl_ref):
+    def step(n, carry):
+        high, low = two_planes(z_ref, n)
+        res = mm(kl_ref[...], jnp.concatenate([high, low, high], axis=0))
+        out_ref[2 * n] = res[:, :128]
+        out_ref[2 * n + 1] = res[:, 128:]
+        return carry
+
+    lax.fori_loop(0, 4, step, 0)
+
+
+def build_frames(at_ref, frames, rows_f32, pick, pick_t, marks_ref):
+    first_plane = (8 * index_of(BLOCK)).astype(F32)
+    first_col = (128 * lax.axis_index("core")).astype(F32)
+    dz, dx = marks_ref[128:129, :], marks_ref[129:130, :]
+
+    def step(a, carry):
+        slot, i = a // 16, lax.rem(a, 16)
+        meta = at_ref[slot, pl.ds(64 + i, 1), :]
+        plane = wrapped(meta[:, 0:1] + dz) - first_plane
+        col = wrapped(meta[:, 2:3] + dx) - first_col
+        mask = jnp.where(plane == marks_ref[0:64, :], marks_ref[64:128, :], 0.0)
+        parts = []
+        for p in range(4):
+            parts.append(mask * at_ref[slot, pl.ds(4 * i + p, 1), :])
+        high, low = split(jnp.concatenate(parts, axis=0))
+        cols = lax.broadcasted_iota(jnp.int32, (128, 128), 0).astype(F32)
+        hit = jnp.where(cols == col, 1.0, 0.0).astype(jnp.bfloat16)
+        res = mm_nt(high, hit) + mm_nt(low, hit)
+        at = pl.ds(pl.multiple_of(8 * a, 8), 8)
+        for p in range(4):
+            for z in range(8):
+                frames[z, p, at, :] = res[64 * p + 8 * z : 64 * p + 8 * z + 8]
+        row = wrapped(meta[:, 1:2] + lax.broadcasted_iota(jnp.int32, (8, 1), 0).astype(F32) - 3.0)
+        ys = lax.broadcasted_iota(jnp.int32, (8, N), 1).astype(F32)
+        rows_f32[at, :] = jnp.where(ys == row, 1.0, 0.0)
+        return carry
+
+    lax.fori_loop(0, 64, step, 0)
+    pick[...] = rows_f32[...].astype(jnp.bfloat16)
+    ys = lax.broadcasted_iota(jnp.int32, (N, 128), 0).astype(F32)
+    for slot in range(4):
+        pick_t[:, 128 * slot : 128 * slot + 128] = jnp.where(
+            ys == at_ref[slot, 80:81, :], 1.0, 0.0
+        ).astype(jnp.bfloat16)
+
+
+def project(z_ref, picked, frames, pick, part):
+    def rows(n, carry):
+        high, low = two_planes(z_ref, n)
+        res = mm(pick[...], high) + mm(pick[...], low)
+        picked[2 * n] = res[:, :128]
+        picked[2 * n + 1] = res[:, 128:]
+        return carry
+
+    lax.fori_loop(0, 4, rows, 0)
+    lanes = lax.broadcasted_iota(jnp.int32, (8, 128), 1)
+
+    def atoms(n, carry):
+        at = pl.ds(pl.multiple_of(64 * n, 64), 64)
+        sums = [jnp.zeros((64, 128), F32) for _ in range(4)]
+        for z in range(8):
+            field = picked[z, at, :]
+            for p in range(4):
+                sums[p] = sums[p] + frames[z, p, at, :] * field
+        value = jnp.zeros((8, 128), F32)
+        for p in range(4):
+            total = jnp.sum(jnp.sum(sums[p].reshape(8, 8, 128), axis=1), axis=1, keepdims=True)
+            value = jnp.where(lanes == p, total, value)
+        part[pl.ds(pl.multiple_of(8 * n, 8), 8), :] = value
+        return carry
+
+    lax.fori_loop(0, 8, atoms, 0)
+
+
+def spread_back(coeffs, picked, frames, pick_t, out_ref):
+    def atoms(n, carry):
+        value = coeffs[pl.ds(pl.multiple_of(8 * n, 8), 8), :]
+        for i in range(8):
+            at = pl.ds(pl.multiple_of(64 * n + 8 * i, 8), 8)
+            wide = [jnp.broadcast_to(value[i : i + 1, p : p + 1], (8, 128)) for p in range(4)]
+            for z in range(8):
+                total = wide[0] * frames[z, 0, at, :]
+                for p in range(1, 4):
+                    total = total + wide[p] * frames[z, p, at, :]
+                picked[z, at, :] = total
+        return carry
+
+    lax.fori_loop(0, 8, atoms, 0)
+
+    def planes(n, carry):
+        high, low = two_planes(picked, n)
+        res = mm(pick_t[...], high) + mm(pick_t[...], low)
+        out_ref[2 * n] += res[:, :128]
+        out_ref[2 * n + 1] += res[:, 128:]
+        return carry
+
+    lax.fori_loop(0, 4, planes, 0)
+
+
+def copy_to(src, dst, send, recv, coords):
+    return pltpu.make_async_remote_copy(
+        src_ref=src, dst_ref=dst, send_sem=send, recv_sem=recv, device_id=coords, device_id_type=MESH
+    )
+
+
+class Swap:
+    def __init__(self, axes, source, target, send, recv):
+        self.args = (axes, source, target, send, recv)
+
+    def start(self):
+        swap_start(*self.args)
+
+    def wait(self):
+        swap_wait(*self.args)
+
+
+def planes_swap(y_ref, z_ref, send, recv):
+    return Swap(
+        BLOCK,
+        lambda peer: y_ref.at[pl.ds(pl.multiple_of(peer * 8, 8), 8)],
+        lambda peer: z_ref.at[:, pl.ds(pl.multiple_of(peer * 8, 8), 8), :],
+        send,
+        recv,
+    )
+
+
+def rows_swap(z_ref, y_ref, send, recv):
+    return Swap(
+        BLOCK,
+        lambda peer: z_ref.at[:, pl.ds(pl.multiple_of(peer * 8, 8), 8), :],
+        lambda peer: y_ref.at[pl.ds(pl.multiple_of(peer * 8, 8), 8)],
+        send,
+        recv,
+    )
+
+
+class Coeffs:
+    def __init__(self, part, got, send, recv):
+        core, me = lax.axis_index("core"), index_of(BLOCK)
+        up, down = lax.rem(me + 1, 32), lax.rem(me + 31, 32)
+        low, high = pl.ds(0, 32), pl.ds(32, 32)
+
+        def place(chip, which):
+            coords = coords_of(BLOCK, chip)
+            coords["core"] = which
+            return coords
+
+        other = {"core": 1 - core}
+        self.coords = [other]
+        self.copies = [copy_to(part.at[low], got.at[0], send.at[0], recv.at[0], other)]
+        self.copies.append(copy_to(part.at[high], got.at[1], send.at[1], recv.at[1], other))
+        for n in range(2):
+            which = lax.rem(core + n, 2)
+            above, below = place(up, which), place(down, which)
+            self.coords += [above, below]
+            slot = 2 + core
+            self.copies.append(copy_to(part.at[high], got.at[slot], send.at[2 + n], recv.at[slot], above))
+            slot = 4 + core
+            self.copies.append(copy_to(part.at[low], got.at[slot], send.at[4 + n], recv.at[slot], below))
+        self.arrivals = [
+            copy_to(part.at[low], got.at[slot], send.at[0], recv.at[slot], other) for slot in range(6)
+        ]
+
+    def greet(self, barrier):
+        for coords in self.coords:
+            pl.semaphore_signal(barrier, inc=1, device_id=coords, device_id_type=MESH)
+        return len(self.coords)
+
+    def start(self):
+        for copy in self.copies:
+            copy.start()
+
+    def wait(self):
+        for copy in self.copies:
+            copy.wait_send()
+        for copy in self.arrivals:
+            copy.wait_recv()
+
+
+def filter_block(
+    cheb_ref, kb_ref, v_ref, pot_ref, at_ref, kl_ref, kr_ref, marks_ref, out_ref,
+    planes, sibs, backs, first, in_rows, in_planes, frames, picked, rows_f32, pick, pick_t, part, got, coeffs,
+    zsend, zrecv, ysend, yrecv, ssend, srecv, csend, crecv,
+):
+    core = lax.axis_index("core")
+    barrier, greeted = greet_group(BLOCK)
+    shares = [Coeffs(part.at[n], got.at[n], csend.at[n], crecv.at[n]) for n in range(2)]
+    greeted = greeted + shares[0].greet(barrier)
+    pl.semaphore_wait(barrier, greeted)
+
+    for n in range(2):
+        x_ref = v_ref if n == 0 else first
+        out = planes_swap(x_ref, planes.at[n], zsend.at[n], zrecv.at[n])
+        sib = copy_to(x_ref, sibs.at[n], ssend.at[n], srecv.at[n], {"core": 1 - core})
+        out.start()
+        sib.start()
+        along_z(x_ref, in_rows, kl_ref)
+        if n == 0:
+            build_frames(at_ref, frames, rows_f32, pick, pick_t, marks_ref)
+        sib.wait()
+        along_x(x_ref, sibs.at[n], pot_ref, in_rows, kr_ref)
+        out.wait()
+        share = shares[n]
+        project(planes.at[n], picked, frames, pick, part.at[n])
+        share.start()
+        along_y(planes.at[n], in_planes.at[n], kl_ref)
+        share.wait()
+        low, high = pl.ds(0, 32), pl.ds(32, 32)
+        own, them = part.at[n], got.at[n]
+        coeffs[low, :] = (own[low, :] + them[0] + them[2] + them[3]) * kb_ref[...]
+        coeffs[high, :] = (own[high, :] + them[1] + them[4] + them[5]) * kb_ref[...]
+        spread_back(coeffs, picked, frames, pick_t, in_planes.at[n])
+        back = rows_swap(in_planes.at[n], backs.at[n], ysend.at[n], yrecv.at[n])
+        back.start()
+        back.wait()
+        if n == 0:
+            def sum_up(k, carry):
+                zs = pl.ds(k * 32, 32)
+                first[zs] = (backs[0, zs] + in_rows[zs]) * 0.25
+                return carry
+        else:
+            def sum_up(k, carry):
+                zs = pl.ds(k * 32, 32)
+                second = 0.5 * (backs[1, zs] + in_rows[zs]) - v_ref[zs]
+                value = cheb_ref[0] * v_ref[zs] + cheb_ref[1] * first[zs] + cheb_ref[2] * second
+                out_ref[zs] = value * value
+                return carry
+
+        lax.fori_loop(0, 8, sum_up, 0)
+
+
+def filter_call(cheb, kb, v, pot, atoms):
+    table = kinetic_table(N)
+    high, low = split3(table)
+    left = np.concatenate([high, high, low], axis=1)
+    side = np.concatenate([table[:128, :128], table[128:, :128]], axis=0)
+    high, low = split3(side)
+    right = np.concatenate([high, high, low], axis=0)
+    off = sphere_offsets()
+    marks = np.zeros((136, 128), np.float32)
+    rows = np.arange(64)[:, None]
+    marks[:64] = rows // 8
+    marks[64:128] = off[None, :, 1] + REACH == rows % 8
+    marks[128] = off[:, 0]
+    marks[129] = off[:, 2]
+    kb_row = jnp.pad(kb, (0, 124)).reshape(1, 128)
+    field = (N, 8, 128)
+    slab = (8, N, 128)
+    vmem = pl.BlockSpec(memory_space=pltpu.VMEM)
+    bf16 = jnp.bfloat16
+    return pl.pallas_call(
+        filter_block,
+        out_shape=jax.ShapeDtypeStruct(field, F32),
+        in_specs=[pl.BlockSpec(memory_space=pltpu.SMEM)] + [vmem] * 7,
+        out_specs=vmem,
+        scratch_shapes=[
+            pltpu.VMEM((2,) + slab, F32),
+            pltpu.VMEM((2,) + field, F32),
+            pltpu.VMEM((2,) + field, F32),
+            pltpu.VMEM(field, F32),
+            pltpu.VMEM(field, F32),
+            pltpu.VMEM((2,) + slab, F32),
+            pltpu.VMEM((8, 4, 512, 128), F32),
+            pltpu.VMEM((8, 512, 128), F32),
+            pltpu.VMEM((512, N), F32),
+            pltpu.VMEM((512, N), bf16),
+            pltpu.VMEM((N, 512), bf16),
+            pltpu.VMEM((2, 64, 128), F32),
+            pltpu.VMEM((2, 6, 32, 128), F32),
+            pltpu.VMEM((64, 128), F32),
+            dma(2, 32), dma(2, 32), dma(2, 32), dma(2, 32), dma(2), dma(2), dma(2, 6), dma(2, 6),
+        ],
+        compiler_params=pltpu.CompilerParams(
+            collective_id=4, has_side_effects=True, vmem_limit_bytes=48 * 1024 * 1024
+        ),
+    )(cheb, kb_row, v, pot, atoms, left, right, marks)
+
+
 def local(random_orbitals, potential, sphere_cells, projectors, kb_energy, cheb_coef):
-    table = kinetic_table(N)
-    chip = index_of(BLOCK)
-    core = lax.axis_index("core")
-
     v_rows, pot_rows = comm_call(
         spread_rows, 1, [(16, 4, 16, N), (2, 4, 16, N)], [dma(16), dma(16), dma(1), dma(2)],
         random_orbitals[0], potential,
@@ -426,57 +660,15 @@
     v, pot = v.reshape(N, 8, 128), pot.reshape(N, 8, 128)
 
     lanes = lax.broadcasted_iota(jnp.int32, (16, 128), 1)
-    centres = sphere_cells[:, :, 0].astype(F32)
-    marks = jnp.where(lanes == 0, centres[:, 0:1], jnp.where(lanes == 1, centres[:, 1:2], 0.0))
-    packed = jnp.concatenate([projectors.reshape(64, SPH), marks], axis=0)
-    (atoms,) = comm_call(spread_atoms, 3, [(4, 80, 128)], [dma(4), dma(4)], packed)
-    proj = atoms[:, :64].reshape(64, 4, SPH)
-    centre_z = atoms[:, 64:, 0].reshape(64).astype(jnp.int32)
-    cell = atoms[:, 64:, 1].reshape(64).astype(jnp.int32)
+    centre_z, cell = sphere_cells[:, 0, :1], sphere_cells[:, 1, :1]
     centre_y, centre_x = cell // N, cell % N
-
-    steps = jnp.arange(8, dtype=jnp.int32) - REACH
-    rows_hit = jnp.arange(N)[None, None, :] == ((centre_y[:, None] + steps) % N)[:, :, None]
-    pick_rows = rows_hit.astype(F32).reshape(512, N)
-    planes_hit = (
-        8 * chip + jnp.arange(8)[None, None, :] == ((centre_z[:, None] + steps) % N)[:, :, None]
-    ).astype(F32)
-    cols_hit = (
-        128 * core + jnp.arange(128)[None, None, :] == ((centre_x[:, None] + steps) % N)[:, :, None]
-    ).astype(F32)
-    cube = jnp.dot(proj.reshape(256, SPH), cube_places(), precision=lax.Precision.HIGHEST)
-    cube = cube.reshape(64, 4, 8, 8, 8)
-    cube = jnp.einsum("apydx,adz->apyzx", cube, planes_hit, precision=lax.Precision.HIGHEST)
-    frames = jnp.einsum("apyzx,axw->apyzw", cube, cols_hit, precision=lax.Precision.HIGHEST)
-
-    def nonlocal_term(planes):
-        picked = jnp.einsum("cy,zyx->czx", pick_rows, planes, precision=HIGH).reshape(64, 1, 8, 8, 128)
-        part = jnp.sum(frames * picked, axis=(2, 3, 4))
-        part = jnp.pad(part.reshape(2, 128), ((0, 6), (0, 0)))
-        (others,) = comm_call(share_coeffs, 4, [(5, 8, 128)], [dma(5), dma(5)], part)
-        low = part[0] + others[0, 0] + others[1, 1] + others[2, 1]
-        high = part[1] + others[0, 1] + others[3, 0] + others[4, 0]
-        coeffs = jnp.concatenate([low, high]).reshape(64, 4) * kb_energy
-        spread = jnp.sum(coeffs[:, :, None, None, None] * frames, axis=1).reshape(512, 8, 128)
-        return jnp.einsum("cy,czx->zyx", pick_rows, spread, precision=HIGH)
-
-    def apply_shifted(rows):
-        planes, sibling = comm_call(
-            to_planes, 5, [(8, N, 128), (32, 8, 8, 128)], [dma(32), dma(32), dma(1), dma(1)],
-            rows.reshape(32, 8, 8, 128),
-        )
-        in_rows = jnp.einsum("wz,zrx->wrx", table, rows, precision=HIGH)
-        in_rows = in_rows + jnp.dot(rows, table[:128, :128], precision=HIGH)
-        in_rows = in_rows + jnp.dot(sibling.reshape(N, 8, 128), table[128:, :128], precision=HIGH)
-        in_rows = in_rows + (pot - 2.0) * rows
-        in_planes = jnp.einsum("wy,zyx->zwx", table, planes, precision=HIGH) + nonlocal_term(planes)
-        (back,) = comm_call(to_rows, 6, [(32, 8, 8, 128)], [dma(32), dma(32)], in_planes)
-        return (back.reshape(N, 8, 128) + in_rows) / 4.0
-
-    first = apply_shifted(v)
-    second = 2.0 * apply_shifted(first) - v
-    filtered = cheb_coef[0] * v + cheb_coef[1] * first + cheb_coef[2] * second
-    squares = (filtered * filtered).reshape(2, 8, 16, 8, 128)
+    meta = jnp.where(lanes == 0, centre_z, jnp.where(lanes == 1, centre_y, centre_x))
+    hit_rows = (centre_y + jnp.arange(8)[None, :] - REACH) % N
+    extra = jnp.broadcast_to(hit_rows.reshape(1, 128), (8, 128))
+    packed = jnp.concatenate([projectors.reshape(64, SPH), meta.astype(F32), extra.astype(F32)], axis=0)
+    (atoms,) = comm_call(spread_atoms, 3, [(4, 88, 128)], [dma(4), dma(4)], packed)
+
+    squares = filter_call(cheb_coef, kb_energy, v, pot, atoms).reshape(2, 8, 16, 8, 128)
     (parts,) = comm_call(gather_squares, 7, [(8, 2, 16, 8, 128)], [dma(8), dma(8)], squares)
     summed = (jnp.sum(parts, axis=0) / 8.0).reshape(2, 2, 2, 4, 8, 128)
     (density,) = comm_call(place_density, 8, [(4, N, N)], [dma(64), dma(64)], summed)

time: 446 us -> 355 us (0.80)
  matrix products: 44.3 us -> 0 us
  local copies, waits for them, and re-layouts: 28.4 us -> 8.07 us
  other arithmetic: 20.6 us -> 2.76 us
  Pallas kernels: 350 us -> 344 us
    pallas_call x11 -> x5, Pallas kernels: 350 us -> 248 us  [comm_call(): pl.pallas_call(kernel, out_shape=[jax.ShapeDtypeStruct(shape, F32) for sh...]
    pallas_call x0 -> x1, Pallas kernels: none -> 95.1 us  [filter_call(): pl.pallas_call(filter_block, out_shape=jax.ShapeDtypeStruct(field, F32),...]
    dot_general x15 -> x0, matrix products: 44.3 us -> none  [the longest x1 10.6 us: local(): jnp.einsum('apydx,adz->apyzx', cube, planes_hit, precision=lax.Precision....]
    reduce_sum x3 -> x0, other arithmetic: 13.7 us -> none  [the longest x2 9.21 us: nonlocal_term(): jnp.sum(coeffs[:, :, None, None, None] * frames, axis=1)]
    dot_general x3 -> x0, local copies, waits for them, and re-layouts: 9.8 us -> none  [the longest x1 7.37 us: local(): jnp.dot(proj.reshape(256, SPH), cube_places(), precision=lax.Precision.HI...]
    squeeze x12 -> x0, local copies, waits for them, and re-layouts: 4.92 us -> none  [the longest x6 2.51 us: nonlocal_term(): low = part[0] + others[0, 0] + others[1, 1] + others[2, 1]]
where the time goes in v2:
time: 355 us
  Pallas kernels  344 us (97%)
  local copies, waits for them, and re-layouts  8.07 us (2%)
    pallas_call x5, Pallas kernels, comm_call(): pl.pallas_call(kernel, out_shape=[jax.ShapeDtypeStruct(shape, F32) for sh...  248 us
    pallas_call x1, Pallas kernels, filter_call(): pl.pallas_call(filter_block, out_shape=jax.ShapeDtypeStruct(field, F32),...  95.1 us

profile of v2, /device:TPU:1, one launch (start us, length us, event | category | flops | bytes accessed | tf_op | source)
XLA Modules:
  0.0 354.5 jit_solution(15649469847523384140)
XLA Ops:
  0.0 0.7 pad_bitcast_fusion.kb_ref
  0.7 19.8 %shard_map.91 = (f32[16,4,16,256]{3,2,1,0:T(8,128)}, f32[2,4,16,256]{3,2,1,0:T(8,128)}) custom-call(f32[4,256,256]{2,1,0:T(8,128)} %bitcast.13, f32[4,256,256]{2,1,0:T(8,128)} %pot_ref.1), custom_call_target="tpu_custom_call" | custom-call | tf_op jit(solution)/shard_map/pallas_call | solution.py:117
  20.5 0.0 copy-start.9
  20.5 0.0 copy-start.8
  20.5 0.0 copy-start.4
  20.5 112.8 %shard_map.92 = (f32[2,32,4,8,128]{4,3,2,1,0:T(8,128)}, f32[2,32,4,8,128]{4,3,2,1,0:T(8,128)}) custom-call(f32[8,2,4,16,256]{4,3,2,1,0:T(8,128)} %bitcast.12, f32[2,4,16,256]{3,2,1,0:T(8,128)} %get-tuple-element.10.pot_ref), custom_call_target="tpu_custom_call" | custom-call | tf_op jit(solution)/shard_map/pallas_call | solution.py:117
  133.3 0.0 copy-start.5
  133.3 0.0 copy-done.9
  133.3 0.7 slice_reduce_fusion.1
  134.0 0.1 add_add_fusion
  134.1 0.1 sub.12
  134.2 0.1 select_convert_fusion
  134.3 0.0 copy-done.8
  134.3 0.6 pad_maximum_fusion.at_ref
  134.9 0.0 copy-start.6
  134.9 0.0 copy-start.7
  134.9 35.6 %shard_map.93.at_ref = f32[4,88,128]{2,1,0:T(8,128)} custom-call(f32[88,128]{1,0:T(8,128)} %pad_maximum_fusion.at_ref), custom_call_target="tpu_custom_call" | custom-call | tf_op jit(solution)/shard_map/pallas_call | solution.py:117
  170.6 0.0 copy-done.4
  170.6 0.0 copy-done.5
  170.6 0.0 copy-done.6
  170.6 0.0 copy-done.7
  170.6 0.0 copy-start.1
  170.6 1.2 copy-done.1
  171.8 0.0 copy-start.2
  171.8 1.2 copy-done.2
  173.1 0.0 copy-start.3
  173.1 0.9 copy-done.3
  174.0 95.1 %shard_map.94 = f32[256,8,128]{2,1,0:T(8,128)S(1)} custom-call(f32[3]{0:T(128)S(1)} %copy-done.7, f32[1,128]{1,0:T(1,128)S(1)} %pad_bitcast_fusion.kb_ref, f32[256,8,128]{2,1,0:T(8,128)S(1)} %bitcast.10, f32[256,8,128]{2,1,0:T(8,128)S(1)} %bitcast.11, f32[4,88,128]{2,1,0:T(8,128)S(1)} %copy-done.3, bf16[256,768]{1,0:T(8,128)(2,1)S(1)} %copy-done.4, ...), custom_call_target="tpu_custom_call" | custom-call | tf_op jit(solution)/shard_map/pallas_call | solution.py:623
  269.1 0.0 copy-start
  269.1 1.0 copy-done
  270.1 55.4 %shard_map.95 = f32[8,2,16,8,128]{4,3,2,1,0:T(8,128)} custom-call(f32[2,8,16,8,128]{4,3,2,1,0:T(8,128)} %bitcast.9), custom_call_target="tpu_custom_call" | custom-call | tf_op jit(solution)/shard_map/pallas_call | solution.py:117
  325.5 1.3 reduce_sum.9
  326.8 0.7 broadcast_multiply_fusion
  327.5 24.8 %shard_map.96 = f32[4,256,256]{2,1,0:T(8,128)} custom-call(f32[2,2,2,4,8,128]{5,4,3,2,1,0:T(8,128)} %bitcast.14), custom_call_target="tpu_custom_call" | custom-call | tf_op jit(solution)/shard_map/pallas_call | solution.py:117
  352.2 2.3 copy.11
  (4 shorter events, 0.0 us)
Async XLA Ops:
  20.5 112.8 %copy-start.9 = (s32[16,2,128]{2,1,0:T(2,128)S(1)}, s32[16,2,128]{2,1,0:T(2,128)}, u32[]{:S(2)}) copy-start(s32[16,2,128]{2,1,0:T(2,128)} %param.11) | copy-start | bytes 49156
  20.5 113.8 %copy-start.8 = (f32[16,4,128]{2,1,0:T(4,128)S(1)}, f32[16,4,128]{2,1,0:T(4,128)}, u32[]{:S(2)}) copy-start(f32[16,4,128]{2,1,0:T(4,128)} %param.12) | copy-start | bytes 98308
  20.5 150.1 %copy-start.4 = (bf16[256,768]{1,0:T(8,128)(2,1)S(1)}, bf16[256,768]{1,0:T(8,128)(2,1)}, u32[]{:S(2)}) copy-start(bf16[256,768]{1,0:T(8,128)(2,1)} %constant.54.clone.kl_ref) | copy-start | bytes 1179652
  133.3 37.3 %copy-start.5 = (bf16[768,128]{1,0:T(8,128)(2,1)S(1)}, bf16[768,128]{1,0:T(8,128)(2,1)}, u32[]{:S(2)}) copy-start(bf16[768,128]{1,0:T(8,128)(2,1)} %constant.55.clone.kr_ref) | copy-start | bytes 589828
  134.9 35.7 %copy-start.6 = (f32[136,128]{1,0:T(8,128)S(1)}, f32[136,128]{1,0:T(8,128)}, u32[]{:S(2)}) copy-start(f32[136,128]{1,0:T(8,128)} %constant.56.clone.marks_ref) | copy-start | bytes 208900
  134.9 35.7 %copy-start.7 = (f32[3]{0:T(128)S(1)}, f32[3]{0:T(128)}, u32[]{:S(2)}) copy-start(f32[3]{0:T(128)} %cheb_ref.1) | copy-start | bytes 40
  170.6 1.2 copy-start.1
  171.8 1.2 copy-start.2
  173.1 0.9 copy-start.3
  269.1 1.0 copy-start

commit v3 on v2

--- a/solution.py
+++ b/solution.py
@@ -113,88 +113,14 @@
     pltpu.make_async_copy(source(me), target(me), recv.at[me]).wait()
 
 
-def comm_call(kernel, cid, outs, scratch, *operands):
-    return pl.pallas_call(
-        kernel,
-        out_shape=[jax.ShapeDtypeStruct(shape, F32) for shape in outs],
-        in_specs=[pl.BlockSpec(memory_space=pl.ANY)] * len(operands),
-        out_specs=[pl.BlockSpec(memory_space=pl.ANY)] * len(outs),
-        scratch_shapes=scratch,
-        compiler_params=pltpu.CompilerParams(collective_id=cid, has_side_effects=True),
-    )(*operands)
+def copy_to(src, dst, send, recv, coords):
+    return pltpu.make_async_remote_copy(
+        src_ref=src, dst_ref=dst, send_sem=send, recv_sem=recv, device_id=coords, device_id_type=MESH
+    )
 
 
 def dma(*shape):
     return pltpu.SemaphoreType.DMA(shape)
-
-
-def spread_rows(v_ref, pot_ref, v_out, pot_out, send, recv, psend, precv):
-    xh = lax.axis_index("xh")
-    me = index_of(PLANE)
-    barrier, greeted = greet_group(PLANE)
-    pl.semaphore_wait(barrier, greeted)
-
-    def source(peer):
-        return v_ref.at[:, pl.ds(pl.multiple_of(peer * 16, 16), 16), :]
-
-    def target(peer):
-        return v_out.at[peer]
-
-    swap_start(PLANE, source, target, send, recv)
-    other = me + 1 - 2 * xh
-    pot_copy = pltpu.make_async_remote_copy(
-        src_ref=pot_ref.at[:, pl.ds(pl.multiple_of(other * 16, 16), 16), :],
-        dst_ref=pot_out.at[xh],
-        send_sem=psend.at[0],
-        recv_sem=precv.at[xh],
-        device_id={"xh": 1 - xh},
-        device_id_type=MESH,
-    )
-    pot_copy.start()
-    own = pltpu.make_async_copy(
-        pot_ref.at[:, pl.ds(pl.multiple_of(me * 16, 16), 16), :], pot_out.at[xh], precv.at[xh]
-    )
-    own.start()
-    swap_wait(PLANE, source, target, send, recv)
-    pot_copy.wait_send()
-    pltpu.make_async_remote_copy(
-        src_ref=pot_ref.at[:, pl.ds(pl.multiple_of(other * 16, 16), 16), :],
-        dst_ref=pot_out.at[1 - xh],
-        send_sem=psend.at[0],
-        recv_sem=precv.at[1 - xh],
-        device_id={"xh": 1 - xh},
-        device_id_type=MESH,
-    ).wait_recv()
-    own.wait()
-
-
-def spread_planes(v_ref, pot_ref, v_out, pot_out, send, recv, psend, precv):
-    barrier, greeted = greet_group(LINE)
-    pl.semaphore_wait(barrier, greeted)
-
-    def cut(peer):
-        rows = pl.ds(pl.multiple_of(lax.rem(peer // 2, 2) * 8, 8), 8)
-        cols = pl.ds(pl.multiple_of(lax.rem(peer, 2) * 128, 128), 128)
-        return rows, cols
-
-    def source(peer):
-        rows, cols = cut(peer)
-        return v_ref.at[peer // 4, :, :, rows, cols]
-
-    def target(peer):
-        return v_out.at[:, peer]
-
-    def pot_source(peer):
-        rows, cols = cut(peer)
-        return pot_ref.at[:, :, rows, cols]
-
-    def pot_target(peer):
-        return pot_out.at[:, peer]
-
-    swap_start(LINE, source, target, send, recv)
-    swap_start(LINE, pot_source, pot_target, psend, precv)
-    swap_wait(LINE, source, target, send, recv)
-    swap_wait(LINE, pot_source, pot_target, psend, precv)
 
 
 def home_of(orbital, slab):
@@ -219,46 +145,43 @@
     return same
 
 
-def spread_atoms(at_ref, at_out, send, recv):
-    slab = index_of(("xh", "zb", "par", "core"))
-    orbital = index_of(("y", "xl"))
-    odd = lax.rem(slab, 2)
-    chip, near = slab // 2, lax.rem(slab // 2 + 2 * odd - 1 + 32, 32)
-    barrier = pltpu.get_barrier_semaphore()
-    mine, zb = index_of(BLOCK), lax.axis_index("zb")
-    own = jnp.int32(0)
-    homes = [home_of(zb, lax.rem(2 * mine - 1 + slot + 64, 64)) for slot in range(4)]
-    sends = []
-    for n, (q, slot) in enumerate(((chip, 1 + odd), (near, 3 - 3 * odd))):
-        for core in range(2):
-            place = coords_of(BLOCK, q)
-            place["zb"] = orbital
-            place["core"] = jnp.int32(core)
-            sends.append((place, slot, 2 * n + core))
-    for home in homes:
-        same = is_me(home)
-        own = own + same.astype(jnp.int32)
-
-        @pl.when(jnp.logical_not(same))
-        def _():
-            pl.semaphore_signal(barrier, inc=1, device_id=full(home), device_id_type=MESH)
-
-    pl.semaphore_wait(barrier, 4 - own)
-
-    def each(go):
-        for place, slot, n in sends:
-            same = is_me(place)
+class Atoms:
+    def __init__(self, at_ref, at_out, send, recv):
+        slab = index_of(("xh", "zb", "par", "core"))
+        orbital = index_of(("y", "xl"))
+        odd = lax.rem(slab, 2)
+        chip, near = slab // 2, lax.rem(slab // 2 + 2 * odd - 1 + 32, 32)
+        mine, zb = index_of(BLOCK), lax.axis_index("zb")
+        self.refs = (at_ref, at_out, send, recv)
+        self.homes = [home_of(zb, lax.rem(2 * mine - 1 + slot + 64, 64)) for slot in range(4)]
+        self.sends = []
+        for n, (q, slot) in enumerate(((chip, 1 + odd), (near, 3 - 3 * odd))):
+            for core in range(2):
+                place = coords_of(BLOCK, q)
+                place["zb"] = orbital
+                place["core"] = jnp.int32(core)
+                self.sends.append((place, slot, 2 * n + core))
+
+    def greet(self, barrier):
+        own = jnp.int32(0)
+        for home in self.homes:
+            same = is_me(home)
+            own = own + same.astype(jnp.int32)
 
             @pl.when(jnp.logical_not(same))
             def _():
-                copy = pltpu.make_async_remote_copy(
-                    src_ref=at_ref,
-                    dst_ref=at_out.at[slot],
-                    send_sem=send.at[n],
-                    recv_sem=recv.at[slot],
-                    device_id=full(place),
-                    device_id_type=MESH,
-                )
+                pl.semaphore_signal(barrier, inc=1, device_id=full(home), device_id_type=MESH)
+
+        return 4 - own
+
+    def each(self, go):
+        at_ref, at_out, send, recv = self.refs
+        for place, slot, n in self.sends:
+            same = is_me(place)
+
+            @pl.when(jnp.logical_not(same))
+            def _():
+                copy = copy_to(at_ref, at_out.at[slot], send.at[n], recv.at[slot], full(place))
                 if go:
                     copy.start()
                 else:
@@ -272,50 +195,16 @@
                 else:
                     copy.wait()
 
-    each(True)
-    each(False)
-    for slot, home in enumerate(homes):
-        @pl.when(jnp.logical_not(is_me(home)))
-        def _():
-            pltpu.make_async_remote_copy(
-                src_ref=at_ref,
-                dst_ref=at_out.at[slot],
-                send_sem=send.at[0],
-                recv_sem=recv.at[slot],
-                device_id=full(home),
-                device_id_type=MESH,
-            ).wait_recv()
-
-
-def gather_squares(f_ref, parts_out, send, recv):
-    axes = ("zb",)
-    barrier, greeted = greet_group(axes)
-    pl.semaphore_wait(barrier, greeted)
-
-    def source(peer):
-        return f_ref.at[:, peer]
-
-    def target(peer):
-        return parts_out.at[peer]
-
-    swap_start(axes, source, target, send, recv)
-    swap_wait(axes, source, target, send, recv)
-
-
-def place_density(s_ref, out_ref, send, recv):
-    barrier, greeted = greet_group(QUAD)
-    pl.semaphore_wait(barrier, greeted)
-
-    def source(peer):
-        return s_ref.at[lax.rem(peer // 4, 2), lax.rem(peer // 2, 2), lax.rem(peer, 2)]
-
-    def target(peer):
-        rows = pl.ds(pl.multiple_of(peer // 2 * 8, 8), 8)
-        cols = pl.ds(pl.multiple_of(lax.rem(peer, 2) * 128, 128), 128)
-        return out_ref.at[:, rows, cols]
-
-    swap_start(QUAD, source, target, send, recv)
-    swap_wait(QUAD, source, target, send, recv)
+    def start(self):
+        self.each(True)
+
+    def wait(self):
+        at_ref, at_out, send, recv = self.refs
+        self.each(False)
+        for slot, home in enumerate(self.homes):
+            @pl.when(jnp.logical_not(is_me(home)))
+            def _():
+                copy_to(at_ref, at_out.at[slot], send.at[0], recv.at[slot], full(home)).wait_recv()
 
 
 def split3(table):
@@ -345,21 +234,27 @@
 def along_z(x_ref, out_ref, kl_ref):
     table = kl_ref[...]
     for pair in range(4):
-        x = jnp.concatenate([x_ref[:, 2 * pair, :], x_ref[:, 2 * pair + 1, :]], axis=1)
+        x = jnp.concatenate(
+            [x_ref[:, :, 2 * pair, :].reshape(N, 128), x_ref[:, :, 2 * pair + 1, :].reshape(N, 128)], axis=1
+        )
         high, low = split(x)
         res = mm(table, jnp.concatenate([high, low, high], axis=0))
-        out_ref[:, 2 * pair, :] = res[:, :128]
-        out_ref[:, 2 * pair + 1, :] = res[:, 128:]
-
-
-def along_x(x_ref, sib_ref, pot_ref, out_ref, kr_ref):
+        out_ref[:, :, 2 * pair, :] = res[:, :128].reshape(2, 128, 128)
+        out_ref[:, :, 2 * pair + 1, :] = res[:, 128:].reshape(2, 128, 128)
+
+
+def planes_at(n):
+    return n // 4, pl.ds(pl.multiple_of(lax.rem(n, 4) * 32, 32), 32)
+
+
+def along_x(x_ref, sib_ref, out_ref, kr_ref):
     def step(n, carry):
-        zs = pl.ds(n * 32, 32)
-        x = x_ref[zs]
-        both = jnp.concatenate([x.reshape(256, 128), sib_ref[zs].reshape(256, 128)], axis=1)
+        half, zs = planes_at(n)
+        x = x_ref[half, zs]
+        both = jnp.concatenate([x.reshape(256, 128), sib_ref[half, zs].reshape(256, 128)], axis=1)
         high, low = split(both)
         res = mm(jnp.concatenate([high, low, high], axis=1), kr_ref[...])
-        out_ref[zs] += res.reshape(32, 8, 128) + (pot_ref[zs] - 2.0) * x
+        out_ref[half, zs] += res.reshape(32, 8, 128) - 2.0 * x
         return carry
 
     lax.fori_loop(0, 8, step, 0)
@@ -469,27 +364,65 @@
     lax.fori_loop(0, 4, planes, 0)
 
 
-def copy_to(src, dst, send, recv, coords):
-    return pltpu.make_async_remote_copy(
-        src_ref=src, dst_ref=dst, send_sem=send, recv_sem=recv, device_id=coords, device_id_type=MESH
-    )
-
-
 class Swap:
     def __init__(self, axes, source, target, send, recv):
-        self.args = (axes, source, target, send, recv)
+        self.axes, self.source, self.target, self.send, self.recv = axes, source, target, send, recv
+        self.me = index_of(axes)
+
+    def remote(self, peer, arriving):
+        return copy_to(
+            self.source(peer),
+            self.target(peer if arriving else self.me),
+            self.send.at[peer],
+            self.recv.at[peer if arriving else self.me],
+            coords_of(self.axes, peer),
+        )
+
+    def own(self):
+        return pltpu.make_async_copy(self.source(self.me), self.target(self.me), self.recv.at[self.me])
 
     def start(self):
-        swap_start(*self.args)
+        swap_start(self.axes, self.source, self.target, self.send, self.recv)
 
     def wait(self):
-        swap_wait(*self.args)
+        swap_wait(self.axes, self.source, self.target, self.send, self.recv)
+
+    def start_one(self, peer):
+        @pl.when(peer != self.me)
+        def _():
+            self.remote(peer, False).start()
+
+        @pl.when(peer == self.me)
+        def _():
+            self.own().start()
+
+    def wait_arrival(self, peer):
+        @pl.when(peer != self.me)
+        def _():
+            self.remote(peer, True).wait_recv()
+
+        @pl.when(peer == self.me)
+        def _():
+            self.own().wait()
+
+    def wait_sends(self):
+        count = group_size(self.axes)
+
+        def step(k, carry):
+            self.remote(lax.rem(self.me + k, count), True).wait_send()
+            return carry
+
+        lax.fori_loop(1, count, step, 0)
+
+
+def planes_of(field, q):
+    return field.at[q // 16, pl.ds(pl.multiple_of(lax.rem(q, 16) * 8, 8), 8)]
 
 
 def planes_swap(y_ref, z_ref, send, recv):
     return Swap(
         BLOCK,
-        lambda peer: y_ref.at[pl.ds(pl.multiple_of(peer * 8, 8), 8)],
+        lambda peer: planes_of(y_ref, peer),
         lambda peer: z_ref.at[:, pl.ds(pl.multiple_of(peer * 8, 8), 8), :],
         send,
         recv,
@@ -500,10 +433,57 @@
     return Swap(
         BLOCK,
         lambda peer: z_ref.at[:, pl.ds(pl.multiple_of(peer * 8, 8), 8), :],
-        lambda peer: y_ref.at[pl.ds(pl.multiple_of(peer * 8, 8), 8)],
+        lambda peer: planes_of(y_ref, peer),
         send,
         recv,
     )
+
+
+def tile_at(rows, cols):
+    return pl.ds(pl.multiple_of(rows * 8, 8), 8), pl.ds(pl.multiple_of(cols * 128, 128), 128)
+
+
+class Ring:
+    def __init__(self, ring, send, recv):
+        self.refs = (ring, send, recv)
+        self.z = index_of(("zb", "par"))
+        self.steps = (8, 7)
+
+    def copy(self, way, step):
+        ring, send, recv = self.refs
+        turn = 1 if way == 0 else 15
+        slot = lax.rem(self.z + (16 - step if way == 0 else step), 16)
+        return copy_to(
+            ring.at[:, slot],
+            ring.at[:, slot],
+            send.at[way, step],
+            recv.at[way, step],
+            coords_of(("zb", "par"), lax.rem(self.z + turn, 16)),
+        )
+
+    def arrival(self, way, step):
+        ring, send, recv = self.refs
+        slot = lax.rem(self.z + (15 - step if way == 0 else step + 1), 16)
+        turn = 1 if way == 0 else 15
+        return copy_to(
+            ring.at[:, slot],
+            ring.at[:, slot],
+            send.at[way, step],
+            recv.at[way, step],
+            coords_of(("zb", "par"), lax.rem(self.z + turn, 16)),
+        )
+
+    def step(self, step):
+        for way in range(2):
+            if 0 < step <= self.steps[way]:
+                self.arrival(way, step - 1).wait_recv()
+            if step < self.steps[way]:
+                self.copy(way, step).start()
+
+    def wait_sends(self):
+        for way in range(2):
+            for step in range(self.steps[way]):
+                self.copy(way, step).wait_send()
 
 
 class Coeffs:
@@ -549,32 +529,153 @@
             copy.wait_recv()
 
 
-def filter_block(
-    cheb_ref, kb_ref, v_ref, pot_ref, at_ref, kl_ref, kr_ref, marks_ref, out_ref,
-    planes, sibs, backs, first, in_rows, in_planes, frames, picked, rows_f32, pick, pick_t, part, got, coeffs,
-    zsend, zrecv, ysend, yrecv, ssend, srecv, csend, crecv,
+def sum_squares(squares, sums, total, send, recv):
+    zb = lax.axis_index("zb")
+    eight = pl.ds(0, 8)
+
+    def flow(way, half, step):
+        turn = 1 if way == 0 else 7
+        place = {"zb": lax.rem(zb + turn, 8)}
+        dst = sums.at[way, half, step]
+        return place, dst, send.at[way, half, step], recv.at[way, half, step]
+
+    def own(way, half, away):
+        chunk = lax.rem(zb + (16 - away if way == 0 else away), 8)
+        return way, pl.ds(pl.multiple_of(chunk * 16 + half * 8, 8), 8)
+
+    flows = [(way, half) for half in range(2) for way in range(2)]
+    for way, half in flows:
+        place, dst, one, two = flow(way, half, 0)
+        copy_to(squares.at[own(way, half, 1)], dst, one, two, place).start()
+
+    def step(n, carry):
+        for way, half in flows:
+            place, dst, one, two = flow(way, half, n)
+            before, src, was_one, was_two = flow(way, half, n - 1)
+            copy_to(src, src, was_one, was_two, before).wait_recv()
+            sums[way, half, n - 1] += squares[own(way, half, n + 1)]
+            copy_to(src, dst, one, two, place).start()
+        return carry
+
+    lax.fori_loop(1, 7, step, 0)
+    for way, half in flows:
+        place, dst, one, two = flow(way, half, 6)
+        copy_to(dst, dst, one, two, place).wait_recv()
+        total[way, 8 * half : 8 * half + 8] = (sums[way, half, 6] + squares[own(way, half, 0)]) * 0.125
+
+    def finish(n, carry):
+        for way, half in flows:
+            place, dst, one, two = flow(way, half, n)
+            copy_to(dst, dst, one, two, place).wait_send()
+        return carry
+
+    lax.fori_loop(0, 7, finish, 0)
+
+
+def program(
+    cheb_ref, kb_ref, orbital_ref, pot_ref, packed_ref, kl_ref, kr_ref, marks_ref, out_ref,
+    v_rows, v, ring_ref, atoms, planes, sibs, backs, first, in_rows, in_planes, frames, picked, rows_f32,
+    pick, pick_t, part, got, coeffs, sums, total,
+    asend, arecv, rsend, rrecv, lsend, lrecv, psend, precv, vsend, vrecv,
+    zsend, zrecv, ysend, yrecv, ssend, srecv, csend, crecv, qsend, qrecv, dsend, drecv,
 ):
-    core = lax.axis_index("core")
-    barrier, greeted = greet_group(BLOCK)
+    core, par, zb, xh = (lax.axis_index(name) for name in ("core", "par", "zb", "xh"))
+    plane_me = index_of(PLANE)
+    z_me = 2 * zb + par
+    barrier, greeted = greet_group(QUAD)
+    greeted = greeted + greet_group(LINE)[1]
+    spread = Atoms(packed_ref, atoms, asend, arecv)
+    greeted = greeted + spread.greet(barrier)
+    pl.semaphore_wait(barrier, greeted)
+
+    to_owner = Swap(
+        PLANE,
+        lambda peer: orbital_ref.at[:, pl.ds(pl.multiple_of(peer * 16, 16), 16), :],
+        lambda peer: v_rows.at[peer],
+        rsend,
+        rrecv,
+    )
+    pot_owner = Swap(
+        ("xh", "core"),
+        lambda peer: pot_ref.at[
+            :,
+            pl.ds(pl.multiple_of((plane_me - xh + peer // 2) * 16, 16), 16),
+            pl.ds(pl.multiple_of(lax.rem(peer, 2) * 128, 128), 128),
+        ],
+        lambda peer: ring_ref.at[peer // 2, z_me, pl.ds(pl.multiple_of(lax.rem(peer, 2) * 4, 4), 4)],
+        psend,
+        precv,
+    )
+    ring = Ring(ring_ref, vsend, vrecv)
+    pot_owner.start()
+    to_owner.start()
+    spread.start()
+    pot_owner.wait()
+    ring.step(0)
+
+    def line_source(peer):
+        rows, cols = tile_at(lax.rem(peer // 2, 2), lax.rem(peer, 2))
+        return v_rows.at[pl.ds(peer // 4 * 2, 2), :, rows, cols]
+
+    line = Swap(
+        LINE, line_source, lambda peer: v.at[:, pl.ds(pl.multiple_of(peer * 4, 4), 4)], lsend, lrecv
+    )
+
+    def to_block(k, carry):
+        there = lax.rem(zb + k, 8)
+        to_owner.wait_arrival(2 * there)
+        to_owner.wait_arrival(2 * there + 1)
+        for n in range(4):
+            line.start_one(4 * there + n)
+        return carry
+
+    lax.fori_loop(0, 8, to_block, 0)
+    ring.step(1)
+    spread.wait()
+    build_frames(atoms, frames, rows_f32, pick, pick_t, marks_ref)
+
+    out = planes_swap(v, planes.at[0], zsend.at[0], zrecv.at[0])
+
+    def arrive(k, carry):
+        there = lax.rem(zb - k + 8, 8)
+        for n in range(4):
+            line.wait_arrival(4 * there + n)
+            if n % 2 == 1:
+                z = 2 * there + n // 2
+                out.start_one(z)
+                out.start_one(16 + z)
+        return carry
+
+    for n in range(4):
+        lax.fori_loop(2 * n, 2 * n + 2, arrive, 0)
+        if n < 3:
+            ring.step(2 + n)
+
     shares = [Coeffs(part.at[n], got.at[n], csend.at[n], crecv.at[n]) for n in range(2)]
-    greeted = greeted + shares[0].greet(barrier)
-    pl.semaphore_wait(barrier, greeted)
+
+    def pot_at(half, n):
+        zs = pl.ds(pl.multiple_of(lax.rem(n, 4) * 4, 4), 4)
+        rows = pl.ds(pl.multiple_of(par * 8, 8), 8)
+        return ring_ref[half, zs, :, rows, :].reshape(32, 8, 128)
 
     for n in range(2):
-        x_ref = v_ref if n == 0 else first
-        out = planes_swap(x_ref, planes.at[n], zsend.at[n], zrecv.at[n])
+        x_ref = v if n == 0 else first
         sib = copy_to(x_ref, sibs.at[n], ssend.at[n], srecv.at[n], {"core": 1 - core})
-        out.start()
+        if n == 1:
+            out = planes_swap(x_ref, planes.at[n], zsend.at[n], zrecv.at[n])
+            out.start()
         sib.start()
         along_z(x_ref, in_rows, kl_ref)
         if n == 0:
-            build_frames(at_ref, frames, rows_f32, pick, pick_t, marks_ref)
+            ring.step(5)
         sib.wait()
-        along_x(x_ref, sibs.at[n], pot_ref, in_rows, kr_ref)
+        along_x(x_ref, sibs.at[n], in_rows, kr_ref)
         out.wait()
         share = shares[n]
         project(planes.at[n], picked, frames, pick, part.at[n])
         share.start()
+        if n == 0:
+            ring.step(6)
         along_y(planes.at[n], in_planes.at[n], kl_ref)
         share.wait()
         low, high = pl.ds(0, 32), pl.ds(32, 32)
@@ -584,24 +685,49 @@
         spread_back(coeffs, picked, frames, pick_t, in_planes.at[n])
         back = rows_swap(in_planes.at[n], backs.at[n], ysend.at[n], yrecv.at[n])
         back.start()
+        if n == 0:
+            ring.step(7)
+            ring.step(8)
         back.wait()
+
         if n == 0:
             def sum_up(k, carry):
-                zs = pl.ds(k * 32, 32)
-                first[zs] = (backs[0, zs] + in_rows[zs]) * 0.25
+                half, zs = planes_at(k)
+                x = v[half, zs]
+                first[half, zs] = (backs[0, half, zs] + in_rows[half, zs] + pot_at(half, k) * x) * 0.25
                 return carry
         else:
             def sum_up(k, carry):
-                zs = pl.ds(k * 32, 32)
-                second = 0.5 * (backs[1, zs] + in_rows[zs]) - v_ref[zs]
-                value = cheb_ref[0] * v_ref[zs] + cheb_ref[1] * first[zs] + cheb_ref[2] * second
-                out_ref[zs] = value * value
+                half, zs = planes_at(k)
+                x, one = v[half, zs], first[half, zs]
+                second = 0.5 * (backs[1, half, zs] + in_rows[half, zs] + pot_at(half, k) * one) - x
+                value = cheb_ref[0] * x + cheb_ref[1] * one + cheb_ref[2] * second
+                in_rows[half, zs] = value * value
                 return carry
 
         lax.fori_loop(0, 8, sum_up, 0)
 
-
-def filter_call(cheb, kb, v, pot, atoms):
+    sum_squares(in_rows, sums, total, qsend, qrecv)
+
+    def density_target(peer):
+        rows, cols = tile_at(peer // 2, lax.rem(peer, 2))
+        return out_ref.at[:, rows, cols]
+
+    done = Swap(
+        QUAD,
+        lambda peer: total.at[lax.rem(peer // 4, 2), pl.ds(pl.multiple_of(lax.rem(peer, 4) * 4, 4), 4)],
+        density_target,
+        dsend,
+        drecv,
+    )
+    done.start()
+    to_owner.wait_sends()
+    line.wait_sends()
+    ring.wait_sends()
+    done.wait()
+
+
+def run(cheb, kb, orbital, pot, packed):
     table = kinetic_table(N)
     high, low = split3(table)
     left = np.concatenate([high, high, low], axis=1)
@@ -616,16 +742,21 @@
     marks[128] = off[:, 0]
     marks[129] = off[:, 2]
     kb_row = jnp.pad(kb, (0, 124)).reshape(1, 128)
-    field = (N, 8, 128)
+    field = (2, 128, 8, 128)
     slab = (8, N, 128)
     vmem = pl.BlockSpec(memory_space=pltpu.VMEM)
+    anywhere = pl.BlockSpec(memory_space=pl.ANY)
     bf16 = jnp.bfloat16
     return pl.pallas_call(
-        filter_block,
-        out_shape=jax.ShapeDtypeStruct(field, F32),
-        in_specs=[pl.BlockSpec(memory_space=pltpu.SMEM)] + [vmem] * 7,
-        out_specs=vmem,
+        program,
+        out_shape=jax.ShapeDtypeStruct((4, N, N), F32),
+        in_specs=[pl.BlockSpec(memory_space=pltpu.SMEM), vmem] + [anywhere] * 3 + [vmem] * 3,
+        out_specs=anywhere,
         scratch_shapes=[
+            pltpu.VMEM((16, 4, 16, N), F32),
+            pltpu.VMEM(field, F32),
+            pltpu.VMEM((2, 16, 8, 16, 128), F32),
+            pltpu.VMEM((4, 88, 128), F32),
             pltpu.VMEM((2,) + slab, F32),
             pltpu.VMEM((2,) + field, F32),
             pltpu.VMEM((2,) + field, F32),
@@ -640,25 +771,19 @@
             pltpu.VMEM((2, 64, 128), F32),
             pltpu.VMEM((2, 6, 32, 128), F32),
             pltpu.VMEM((64, 128), F32),
+            pltpu.VMEM((2, 2, 7, 8, 8, 128), F32),
+            pltpu.VMEM((2, 16, 8, 128), F32),
+            dma(4), dma(4), dma(16), dma(16), dma(32), dma(32), dma(4), dma(4), dma(2, 8), dma(2, 8),
             dma(2, 32), dma(2, 32), dma(2, 32), dma(2, 32), dma(2), dma(2), dma(2, 6), dma(2, 6),
+            dma(2, 2, 7), dma(2, 2, 7), dma(64), dma(64),
         ],
         compiler_params=pltpu.CompilerParams(
-            collective_id=4, has_side_effects=True, vmem_limit_bytes=48 * 1024 * 1024
+            collective_id=1, has_side_effects=True, vmem_limit_bytes=61 * 1024 * 1024
         ),
-    )(cheb, kb_row, v, pot, atoms, left, right, marks)
+    )(cheb, kb_row, orbital, pot, packed, left, right, marks)
 
 
 def local(random_orbitals, potential, sphere_cells, projectors, kb_energy, cheb_coef):
-    v_rows, pot_rows = comm_call(
-        spread_rows, 1, [(16, 4, 16, N), (2, 4, 16, N)], [dma(16), dma(16), dma(1), dma(2)],
-        random_orbitals[0], potential,
-    )
-    v, pot = comm_call(
-        spread_planes, 2, [(2, 32, 4, 8, 128)] * 2, [dma(32)] * 4,
-        v_rows.reshape(8, 2, 4, 16, N), pot_rows,
-    )
-    v, pot = v.reshape(N, 8, 128), pot.reshape(N, 8, 128)
-
     lanes = lax.broadcasted_iota(jnp.int32, (16, 128), 1)
     centre_z, cell = sphere_cells[:, 0, :1], sphere_cells[:, 1, :1]
     centre_y, centre_x = cell // N, cell % N
@@ -666,13 +791,7 @@
     hit_rows = (centre_y + jnp.arange(8)[None, :] - REACH) % N
     extra = jnp.broadcast_to(hit_rows.reshape(1, 128), (8, 128))
     packed = jnp.concatenate([projectors.reshape(64, SPH), meta.astype(F32), extra.astype(F32)], axis=0)
-    (atoms,) = comm_call(spread_atoms, 3, [(4, 88, 128)], [dma(4), dma(4)], packed)
-
-    squares = filter_call(cheb_coef, kb_energy, v, pot, atoms).reshape(2, 8, 16, 8, 128)
-    (parts,) = comm_call(gather_squares, 7, [(8, 2, 16, 8, 128)], [dma(8), dma(8)], squares)
-    summed = (jnp.sum(parts, axis=0) / 8.0).reshape(2, 2, 2, 4, 8, 128)
-    (density,) = comm_call(place_density, 8, [(4, N, N)], [dma(64), dma(64)], summed)
-    return density
+    return run(cheb_coef, kb_energy, random_orbitals[0], potential, packed)
 
 
 def solution(mesh):

time: 355 us -> 247 us (0.70)
  Pallas kernels: 344 us -> 240 us
    pallas_call x6 -> x1, Pallas kernels: 344 us -> 240 us  [run(): pl.pallas_call(program, out_shape=jax.ShapeDtypeStruct((4, N, N), F32), i...]
    unnamed x21 -> x5, local copies, waits for them, and re-layouts: 6.65 us -> 2.94 us
where the time goes in v3:
time: 247 us; the launch traced here: 246 us
  Pallas kernels  240 us (97%)
  local copies, waits for them, and re-layouts  5.08 us (2%)
    pallas_call x1, Pallas kernels, run(): pl.pallas_call(program, out_shape=jax.ShapeDtypeStruct((4, N, N), F32), i...  240 us

profile of v3, /device:TPU:1, one launch (start us, length us, event | category | flops | bytes accessed | tf_op | source)
XLA Modules:
  0.0 246.3 jit_solution(10851691424872417304)
XLA Ops:
  0.0 0.0 copy-start.1
  0.0 0.7 copy-done.1
  0.7 0.6 pad_bitcast_fusion.kb_ref
  1.2 0.0 copy-start
  1.2 1.5 slice_reduce_fusion.1
  2.7 0.1 select_convert_fusion
  2.8 0.1 add_add_fusion
  2.9 0.1 sub.12
  3.0 0.0 copy-done
  3.0 0.6 pad_maximum_fusion.packed_ref
  3.6 240.4 %shard_map.91 = f32[4,256,256]{2,1,0:T(8,128)} custom-call(f32[3]{0:T(128)} %cheb_ref.1, f32[1,128]{1,0:T(1,128)} %pad_bitcast_fusion.kb_ref, f32[4,256,256]{2,1,0:T(8,128)} %bitcast.4, f32[4,256,256]{2,1,0:T(8,128)} %pot_ref.1, f32[88,128]{1,0:T(8,128)} %pad_maximum_fusion.packed_ref, bf16[256,768]{1,0:T(8,128)(2,1)} %constant.50.clone.kl_ref, ...), custom_call_target="tpu_custom_call" | custom-call | tf_op jit(solution)/shard_map/pallas_call | solution.py:750
  244.0 2.3 copy.11
  (4 shorter events, 0.0 us)
Async XLA Ops:
  0.0 0.7 copy-start.1
  1.2 1.8 copy-start

commit v4 on v3

--- a/solution.py
+++ b/solution.py
@@ -73,46 +73,6 @@
     return barrier, count - 1
 
 
-def swap_start(axes, source, target, send, recv):
-    me, count = index_of(axes), group_size(axes)
-
-    def step(k, carry):
-        peer = lax.rem(me + k, count)
-        pltpu.make_async_remote_copy(
-            src_ref=source(peer),
-            dst_ref=target(me),
-            send_sem=send.at[peer],
-            recv_sem=recv.at[me],
-            device_id=coords_of(axes, peer),
-            device_id_type=MESH,
-        ).start()
-        return carry
-
-    lax.fori_loop(1, count, step, 0)
-    pltpu.make_async_copy(source(me), target(me), recv.at[me]).start()
-
-
-def swap_wait(axes, source, target, send, recv):
-    me, count = index_of(axes), group_size(axes)
-
-    def step(k, carry):
-        peer = lax.rem(me + k, count)
-        copy = pltpu.make_async_remote_copy(
-            src_ref=source(peer),
-            dst_ref=target(peer),
-            send_sem=send.at[peer],
-            recv_sem=recv.at[peer],
-            device_id=coords_of(axes, peer),
-            device_id_type=MESH,
-        )
-        copy.wait_send()
-        copy.wait_recv()
-        return carry
-
-    lax.fori_loop(1, count, step, 0)
-    pltpu.make_async_copy(source(me), target(me), recv.at[me]).wait()
-
-
 def copy_to(src, dst, send, recv, coords):
     return pltpu.make_async_remote_copy(
         src_ref=src, dst_ref=dst, send_sem=send, recv_sem=recv, device_id=coords, device_id_type=MESH
@@ -123,7 +83,12 @@
     return pltpu.SemaphoreType.DMA(shape)
 
 
-def home_of(orbital, slab):
+def wait_all(ref, sem):
+    pltpu.make_async_copy(ref, ref, sem).wait()
+
+
+def home_of(block, slab):
+    orbital = lax.rem(block + 16 - lax.rem(slab // 2, 16), 8)
     return {
         "y": orbital // 2,
         "xl": lax.rem(orbital, 2),
@@ -145,10 +110,23 @@
     return same
 
 
+def pack_atoms(cells_ref, proj_ref, packed):
+    packed[0:64, :] = proj_ref[...]
+    lanes = lax.broadcasted_iota(jnp.int32, (16, 128), 1)
+    centre_z, cell = cells_ref[:, 0, :][:, 0:1], cells_ref[:, 1, :][:, 0:1]
+    centre_y, centre_x = cell // N, lax.rem(cell, N)
+    meta = jnp.where(lanes == 0, centre_z, jnp.where(lanes == 1, centre_y, centre_x))
+    packed[64:80, :] = meta.astype(F32)
+    atom = lax.broadcasted_iota(jnp.int32, (16, 128), 0)
+    mine = jnp.sum(jnp.where(lanes // 8 == atom, centre_y, 0).astype(F32), axis=0, keepdims=True)
+    step = lax.rem(lanes[0:1], 8).astype(F32) - REACH
+    packed[80:88, :] = jnp.broadcast_to(wrapped(mine + step), (8, 128))
+
+
 class Atoms:
     def __init__(self, at_ref, at_out, send, recv):
         slab = index_of(("xh", "zb", "par", "core"))
-        orbital = index_of(("y", "xl"))
+        there = lax.rem(index_of(("y", "xl")) + index_of(("zb", "par")), 8)
         odd = lax.rem(slab, 2)
         chip, near = slab // 2, lax.rem(slab // 2 + 2 * odd - 1 + 32, 32)
         mine, zb = index_of(BLOCK), lax.axis_index("zb")
@@ -158,7 +136,7 @@
         for n, (q, slot) in enumerate(((chip, 1 + odd), (near, 3 - 3 * odd))):
             for core in range(2):
                 place = coords_of(BLOCK, q)
-                place["zb"] = orbital
+                place["zb"] = there
                 place["core"] = jnp.int32(core)
                 self.sends.append((place, slot, 2 * n + core))
 
@@ -365,58 +343,47 @@
 
 
 class Swap:
-    def __init__(self, axes, source, target, send, recv):
+    def __init__(self, axes, source, target, send, recv, each=False):
         self.axes, self.source, self.target, self.send, self.recv = axes, source, target, send, recv
-        self.me = index_of(axes)
-
-    def remote(self, peer, arriving):
+        self.me, self.each = index_of(axes), each
+
+    def arrived(self, peer):
+        return self.recv.at[peer] if self.each else self.recv
+
+    def remote(self, peer):
         return copy_to(
-            self.source(peer),
-            self.target(peer if arriving else self.me),
-            self.send.at[peer],
-            self.recv.at[peer if arriving else self.me],
-            coords_of(self.axes, peer),
+            self.source(peer), self.target(self.me), self.send, self.arrived(self.me), coords_of(self.axes, peer)
         )
 
     def own(self):
-        return pltpu.make_async_copy(self.source(self.me), self.target(self.me), self.recv.at[self.me])
+        return pltpu.make_async_copy(self.source(self.me), self.target(self.me), self.arrived(self.me))
 
     def start(self):
-        swap_start(self.axes, self.source, self.target, self.send, self.recv)
-
-    def wait(self):
-        swap_wait(self.axes, self.source, self.target, self.send, self.recv)
+        count = group_size(self.axes)
+
+        def step(k, carry):
+            self.remote(lax.rem(self.me + k, count)).start()
+            return carry
+
+        lax.fori_loop(1, count, step, 0)
+        self.own().start()
 
     def start_one(self, peer):
         @pl.when(peer != self.me)
         def _():
-            self.remote(peer, False).start()
+            self.remote(peer).start()
 
         @pl.when(peer == self.me)
         def _():
             self.own().start()
 
-    def wait_arrival(self, peer):
-        @pl.when(peer != self.me)
-        def _():
-            self.remote(peer, True).wait_recv()
-
-        @pl.when(peer == self.me)
-        def _():
-            self.own().wait()
-
-    def wait_sends(self):
-        count = group_size(self.axes)
-
-        def step(k, carry):
-            self.remote(lax.rem(self.me + k, count), True).wait_send()
-            return carry
-
-        lax.fori_loop(1, count, step, 0)
-
 
 def planes_of(field, q):
     return field.at[q // 16, pl.ds(pl.multiple_of(lax.rem(q, 16) * 8, 8), 8)]
+
+
+def sent_31(field):
+    return field.at[:, pl.ds(0, 124)]
 
 
 def planes_swap(y_ref, z_ref, send, recv):
@@ -456,7 +423,7 @@
         return copy_to(
             ring.at[:, slot],
             ring.at[:, slot],
-            send.at[way, step],
+            send,
             recv.at[way, step],
             coords_of(("zb", "par"), lax.rem(self.z + turn, 16)),
         )
@@ -468,7 +435,7 @@
         return copy_to(
             ring.at[:, slot],
             ring.at[:, slot],
-            send.at[way, step],
+            send,
             recv.at[way, step],
             coords_of(("zb", "par"), lax.rem(self.z + turn, 16)),
         )
@@ -481,9 +448,8 @@
                 self.copy(way, step).start()
 
     def wait_sends(self):
-        for way in range(2):
-            for step in range(self.steps[way]):
-                self.copy(way, step).wait_send()
+        ring, send, _ = self.refs
+        wait_all(ring.at[:, pl.ds(0, 15)], send)
 
 
 class Coeffs:
@@ -498,35 +464,26 @@
             return coords
 
         other = {"core": 1 - core}
-        self.coords = [other]
-        self.copies = [copy_to(part.at[low], got.at[0], send.at[0], recv.at[0], other)]
-        self.copies.append(copy_to(part.at[high], got.at[1], send.at[1], recv.at[1], other))
+        self.refs = (got, send, recv)
+        self.coords = []
+        self.copies = [copy_to(part.at[low], got.at[0], send, recv, other)]
+        self.copies.append(copy_to(part.at[high], got.at[1], send, recv, other))
         for n in range(2):
             which = lax.rem(core + n, 2)
             above, below = place(up, which), place(down, which)
-            self.coords += [above, below]
-            slot = 2 + core
-            self.copies.append(copy_to(part.at[high], got.at[slot], send.at[2 + n], recv.at[slot], above))
-            slot = 4 + core
-            self.copies.append(copy_to(part.at[low], got.at[slot], send.at[4 + n], recv.at[slot], below))
-        self.arrivals = [
-            copy_to(part.at[low], got.at[slot], send.at[0], recv.at[slot], other) for slot in range(6)
-        ]
-
-    def greet(self, barrier):
-        for coords in self.coords:
-            pl.semaphore_signal(barrier, inc=1, device_id=coords, device_id_type=MESH)
-        return len(self.coords)
+            if n == 1:
+                self.coords = [above, below]
+            self.copies.append(copy_to(part.at[high], got.at[2 + core], send, recv, above))
+            self.copies.append(copy_to(part.at[low], got.at[4 + core], send, recv, below))
 
     def start(self):
         for copy in self.copies:
             copy.start()
 
     def wait(self):
-        for copy in self.copies:
-            copy.wait_send()
-        for copy in self.arrivals:
-            copy.wait_recv()
+        got, send, recv = self.refs
+        wait_all(got, recv)
+        wait_all(got, send)
 
 
 def sum_squares(squares, sums, total, send, recv):
@@ -537,7 +494,7 @@
         turn = 1 if way == 0 else 7
         place = {"zb": lax.rem(zb + turn, 8)}
         dst = sums.at[way, half, step]
-        return place, dst, send.at[way, half, step], recv.at[way, half, step]
+        return place, dst, send, recv.at[way, half, step]
 
     def own(way, half, away):
         chunk = lax.rem(zb + (16 - away if way == 0 else away), 8)
@@ -563,37 +520,35 @@
         copy_to(dst, dst, one, two, place).wait_recv()
         total[way, 8 * half : 8 * half + 8] = (sums[way, half, 6] + squares[own(way, half, 0)]) * 0.125
 
-    def finish(n, carry):
-        for way, half in flows:
-            place, dst, one, two = flow(way, half, n)
-            copy_to(dst, dst, one, two, place).wait_send()
-        return carry
-
-    lax.fori_loop(0, 7, finish, 0)
+    wait_all(sums, send)
 
 
 def program(
-    cheb_ref, kb_ref, orbital_ref, pot_ref, packed_ref, kl_ref, kr_ref, marks_ref, out_ref,
-    v_rows, v, ring_ref, atoms, planes, sibs, backs, first, in_rows, in_planes, frames, picked, rows_f32,
-    pick, pick_t, part, got, coeffs, sums, total,
+    cheb_ref, kb_ref, orbital_ref, pot_ref, cells_ref, proj_ref, kl_ref, kr_ref, marks_ref, out_ref,
+    packed, v_rows, v, ring_ref, atoms, planes, sibs, backs, first, in_rows, in_planes, frames, picked, rows_f32,
+    pick, pick_t, part, got, coeffs, sums, total, quad,
     asend, arecv, rsend, rrecv, lsend, lrecv, psend, precv, vsend, vrecv,
     zsend, zrecv, ysend, yrecv, ssend, srecv, csend, crecv, qsend, qrecv, dsend, drecv,
 ):
     core, par, zb, xh = (lax.axis_index(name) for name in ("core", "par", "zb", "xh"))
     plane_me = index_of(PLANE)
     z_me = 2 * zb + par
-    barrier, greeted = greet_group(QUAD)
-    greeted = greeted + greet_group(LINE)[1]
-    spread = Atoms(packed_ref, atoms, asend, arecv)
+    shares = [Coeffs(part.at[n], got.at[n], csend.at[n], crecv.at[n]) for n in range(2)]
+    barrier, greeted = greet_group(BLOCK)
+    greeted = greeted + greet_group(LINE)[1] + 3
+    for coords in shares[0].coords + [{"xh": 1 - xh, "core": 1 - core}]:
+        pl.semaphore_signal(barrier, inc=1, device_id=coords, device_id_type=MESH)
+    spread = Atoms(packed, atoms, asend, arecv)
     greeted = greeted + spread.greet(barrier)
+    pack_atoms(cells_ref, proj_ref, packed)
     pl.semaphore_wait(barrier, greeted)
 
     to_owner = Swap(
         PLANE,
         lambda peer: orbital_ref.at[:, pl.ds(pl.multiple_of(peer * 16, 16), 16), :],
         lambda peer: v_rows.at[peer],
-        rsend,
-        rrecv,
+        rsend.at[0],
+        rrecv.at[0],
     )
     pot_owner = Swap(
         ("xh", "core"),
@@ -603,34 +558,36 @@
             pl.ds(pl.multiple_of(lax.rem(peer, 2) * 128, 128), 128),
         ],
         lambda peer: ring_ref.at[peer // 2, z_me, pl.ds(pl.multiple_of(lax.rem(peer, 2) * 4, 4), 4)],
-        psend,
-        precv,
-    )
-    ring = Ring(ring_ref, vsend, vrecv)
+        psend.at[0],
+        precv.at[0],
+    )
+    ring = Ring(ring_ref, vsend.at[0], vrecv)
     pot_owner.start()
     to_owner.start()
     spread.start()
-    pot_owner.wait()
+    wait_all(ring_ref.at[:, z_me], precv.at[0])
     ring.step(0)
+    ring.step(1)
 
     def line_source(peer):
         rows, cols = tile_at(lax.rem(peer // 2, 2), lax.rem(peer, 2))
         return v_rows.at[pl.ds(peer // 4 * 2, 2), :, rows, cols]
 
     line = Swap(
-        LINE, line_source, lambda peer: v.at[:, pl.ds(pl.multiple_of(peer * 4, 4), 4)], lsend, lrecv
+        LINE,
+        line_source,
+        lambda peer: v.at[:, pl.ds(pl.multiple_of(peer * 4, 4), 4)],
+        lsend.at[0], lrecv, True,
     )
 
     def to_block(k, carry):
         there = lax.rem(zb + k, 8)
-        to_owner.wait_arrival(2 * there)
-        to_owner.wait_arrival(2 * there + 1)
         for n in range(4):
             line.start_one(4 * there + n)
         return carry
 
+    wait_all(v_rows, rrecv.at[0])
     lax.fori_loop(0, 8, to_block, 0)
-    ring.step(1)
     spread.wait()
     build_frames(atoms, frames, rows_f32, pick, pick_t, marks_ref)
 
@@ -639,19 +596,20 @@
     def arrive(k, carry):
         there = lax.rem(zb - k + 8, 8)
         for n in range(4):
-            line.wait_arrival(4 * there + n)
+            wait_all(line.target(4 * there + n), lrecv.at[4 * there + n])
             if n % 2 == 1:
                 z = 2 * there + n // 2
                 out.start_one(z)
                 out.start_one(16 + z)
         return carry
 
-    for n in range(4):
-        lax.fori_loop(2 * n, 2 * n + 2, arrive, 0)
-        if n < 3:
-            ring.step(2 + n)
-
-    shares = [Coeffs(part.at[n], got.at[n], csend.at[n], crecv.at[n]) for n in range(2)]
+    lax.fori_loop(0, 8, arrive, 0)
+    ring.step(2)
+
+    lanes = lax.broadcasted_iota(jnp.int32, (1, 128), 1)
+    energies = jnp.zeros((1, 128), F32)
+    for p in range(4):
+        energies = jnp.where(lanes == p, kb_ref[p], energies)
 
     def pot_at(half, n):
         zs = pl.ds(pl.multiple_of(lax.rem(n, 4) * 4, 4), 4)
@@ -667,28 +625,32 @@
         sib.start()
         along_z(x_ref, in_rows, kl_ref)
         if n == 0:
-            ring.step(5)
+            ring.step(3)
         sib.wait()
         along_x(x_ref, sibs.at[n], in_rows, kr_ref)
-        out.wait()
+        if n == 0:
+            ring.step(4)
+        wait_all(planes.at[n], zrecv.at[n])
         share = shares[n]
         project(planes.at[n], picked, frames, pick, part.at[n])
         share.start()
         if n == 0:
-            ring.step(6)
+            ring.step(5)
         along_y(planes.at[n], in_planes.at[n], kl_ref)
         share.wait()
+        if n == 0:
+            ring.step(6)
         low, high = pl.ds(0, 32), pl.ds(32, 32)
         own, them = part.at[n], got.at[n]
-        coeffs[low, :] = (own[low, :] + them[0] + them[2] + them[3]) * kb_ref[...]
-        coeffs[high, :] = (own[high, :] + them[1] + them[4] + them[5]) * kb_ref[...]
+        coeffs[low, :] = (own[low, :] + them[0] + them[2] + them[3]) * energies
+        coeffs[high, :] = (own[high, :] + them[1] + them[4] + them[5]) * energies
         spread_back(coeffs, picked, frames, pick_t, in_planes.at[n])
         back = rows_swap(in_planes.at[n], backs.at[n], ysend.at[n], yrecv.at[n])
         back.start()
         if n == 0:
             ring.step(7)
             ring.step(8)
-        back.wait()
+        wait_all(backs.at[n], yrecv.at[n])
 
         if n == 0:
             def sum_up(k, carry):
@@ -707,27 +669,42 @@
 
         lax.fori_loop(0, 8, sum_up, 0)
 
-    sum_squares(in_rows, sums, total, qsend, qrecv)
-
-    def density_target(peer):
+    sum_squares(in_rows, sums, total, qsend.at[0], qrecv)
+
+    def quad_target(peer):
         rows, cols = tile_at(peer // 2, lax.rem(peer, 2))
-        return out_ref.at[:, rows, cols]
-
+        return quad.at[:, :, rows, cols]
+
+    to_core = Swap(
+        ("par", "core"),
+        lambda peer: total.at[:, pl.ds(pl.multiple_of(peer * 4, 4), 4)],
+        quad_target,
+        dsend.at[0],
+        drecv.at[0],
+    )
+    to_core.start()
+    wait_all(quad, drecv.at[0])
     done = Swap(
-        QUAD,
-        lambda peer: total.at[lax.rem(peer // 4, 2), pl.ds(pl.multiple_of(lax.rem(peer, 4) * 4, 4), 4)],
-        density_target,
-        dsend,
-        drecv,
+        PLANE,
+        lambda peer: quad.at[lax.rem(peer, 2)],
+        lambda peer: out_ref.at[:, pl.ds(pl.multiple_of(peer * 16, 16), 16), :],
+        dsend.at[1],
+        drecv.at[1],
     )
     done.start()
-    to_owner.wait_sends()
-    line.wait_sends()
+    wait_all(v_rows.at[pl.ds(0, 15)], rsend.at[0])
+    wait_all(ring_ref.at[0, pl.ds(0, 12), 0], psend.at[0])
+    wait_all(sent_31(v), lsend.at[0])
     ring.wait_sends()
-    done.wait()
-
-
-def run(cheb, kb, orbital, pot, packed):
+    for n in range(2):
+        wait_all(sent_31(v), zsend.at[n])
+        wait_all(sent_31(v), ysend.at[n])
+    wait_all(total.at[:, pl.ds(0, 12)], dsend.at[0])
+    wait_all(v_rows.at[pl.ds(0, 15)], dsend.at[1])
+    wait_all(out_ref, drecv.at[1])
+
+
+def run(cheb, kb, orbital, pot, cells, proj):
     table = kinetic_table(N)
     high, low = split3(table)
     left = np.concatenate([high, high, low], axis=1)
@@ -741,18 +718,19 @@
     marks[64:128] = off[None, :, 1] + REACH == rows % 8
     marks[128] = off[:, 0]
     marks[129] = off[:, 2]
-    kb_row = jnp.pad(kb, (0, 124)).reshape(1, 128)
     field = (2, 128, 8, 128)
     slab = (8, N, 128)
     vmem = pl.BlockSpec(memory_space=pltpu.VMEM)
-    anywhere = pl.BlockSpec(memory_space=pl.ANY)
+    smem = pl.BlockSpec(memory_space=pltpu.SMEM)
+    hbm = pl.BlockSpec(memory_space=pltpu.HBM)
     bf16 = jnp.bfloat16
     return pl.pallas_call(
         program,
         out_shape=jax.ShapeDtypeStruct((4, N, N), F32),
-        in_specs=[pl.BlockSpec(memory_space=pltpu.SMEM), vmem] + [anywhere] * 3 + [vmem] * 3,
-        out_specs=anywhere,
+        in_specs=[smem] * 2 + [hbm] * 2 + [vmem] * 5,
+        out_specs=pl.BlockSpec(memory_space=pl.ANY),
         scratch_shapes=[
+            pltpu.VMEM((88, 128), F32),
             pltpu.VMEM((16, 4, 16, N), F32),
             pltpu.VMEM(field, F32),
             pltpu.VMEM((2, 16, 8, 16, 128), F32),
@@ -773,25 +751,22 @@
             pltpu.VMEM((64, 128), F32),
             pltpu.VMEM((2, 2, 7, 8, 8, 128), F32),
             pltpu.VMEM((2, 16, 8, 128), F32),
-            dma(4), dma(4), dma(16), dma(16), dma(32), dma(32), dma(4), dma(4), dma(2, 8), dma(2, 8),
-            dma(2, 32), dma(2, 32), dma(2, 32), dma(2, 32), dma(2), dma(2), dma(2, 6), dma(2, 6),
-            dma(2, 2, 7), dma(2, 2, 7), dma(64), dma(64),
+            pltpu.VMEM((2, 4, 16, N), F32),
+            dma(4), dma(4), dma(1), dma(1), dma(1), dma(32), dma(1), dma(1), dma(1), dma(2, 8),
+            dma(2), dma(2), dma(2), dma(2), dma(2), dma(2), dma(2), dma(2),
+            dma(1), dma(2, 2, 7), dma(2), dma(2),
         ],
         compiler_params=pltpu.CompilerParams(
-            collective_id=1, has_side_effects=True, vmem_limit_bytes=61 * 1024 * 1024
+            collective_id=1, has_side_effects=True, vmem_limit_bytes=62 * 1024 * 1024
         ),
-    )(cheb, kb_row, orbital, pot, packed, left, right, marks)
+    )(cheb, kb, orbital, pot, cells, proj, left, right, marks)
 
 
 def local(random_orbitals, potential, sphere_cells, projectors, kb_energy, cheb_coef):
-    lanes = lax.broadcasted_iota(jnp.int32, (16, 128), 1)
-    centre_z, cell = sphere_cells[:, 0, :1], sphere_cells[:, 1, :1]
-    centre_y, centre_x = cell // N, cell % N
-    meta = jnp.where(lanes == 0, centre_z, jnp.where(lanes == 1, centre_y, centre_x))
-    hit_rows = (centre_y + jnp.arange(8)[None, :] - REACH) % N
-    extra = jnp.broadcast_to(hit_rows.reshape(1, 128), (8, 128))
-    packed = jnp.concatenate([projectors.reshape(64, SPH), meta.astype(F32), extra.astype(F32)], axis=0)
-    return run(cheb_coef, kb_energy, random_orbitals[0], potential, packed)
+    return run(
+        cheb_coef, kb_energy, random_orbitals[0], potential, sphere_cells,
+        projectors.reshape(4 * projectors.shape[0], SPH),
+    )
 
 
 def solution(mesh):

time: 247 us -> 234 us (0.947)
  Pallas kernels: 240 us -> 231 us
  local copies, waits for them, and re-layouts: 5.08 us -> 2.29 us
    pallas_call x1, Pallas kernels: 240 us -> 231 us  [run(): pl.pallas_call(program, out_shape=jax.ShapeDtypeStruct((4, N, N), F32), i...]
where the time goes in v4:
time: 234 us; the launch traced here: 233 us
  Pallas kernels  231 us (99%)
    pallas_call x1, Pallas kernels, run(): pl.pallas_call(program, out_shape=jax.ShapeDtypeStruct((4, N, N), F32), i...  231 us

profile of v4, /device:TPU:1, one launch (start us, length us, event | category | flops | bytes accessed | tf_op | source)
XLA Modules:
  0.0 233.4 jit_solution(4299772663039528834)
XLA Ops:
  0.0 231.1 %shard_map.91 = f32[4,256,256]{2,1,0:T(8,128)} custom-call(f32[3]{0:T(128)} %cheb_ref.1, f32[4]{0:T(128)} %kb_ref.1, f32[4,256,256]{2,1,0:T(8,128)} %bitcast.2, f32[4,256,256]{2,1,0:T(8,128)} %pot_ref.1, s32[16,2,128]{2,1,0:T(2,128)} %cells_ref.1, f32[64,128]{1,0:T(8,128)} %bitcast.3, bf16[256,768]{1,0:T(8,128)(2,1)} %constant.6.clone.kl_ref, ...), custom_call_target="tpu_custom_call" | custom-call | tf_op jit(solution)/shard_map/pallas_call | solution.py:727
  231.1 2.3 copy.11

commit v5 on v4

--- a/solution.py
+++ b/solution.py
@@ -236,6 +236,9 @@
         return carry
 
     lax.fori_loop(0, 8, step, 0)
+
+
+REACHED = (range(0, 3), range(0, 7), range(1, 8), range(5, 8))
 
 
 def two_planes(z_ref, n):
@@ -300,10 +303,10 @@
     lax.fori_loop(0, 4, rows, 0)
     lanes = lax.broadcasted_iota(jnp.int32, (8, 128), 1)
 
-    def atoms(n, carry):
+    def atoms(planes, n, carry):
         at = pl.ds(pl.multiple_of(64 * n, 64), 64)
         sums = [jnp.zeros((64, 128), F32) for _ in range(4)]
-        for z in range(8):
+        for z in planes:
             field = picked[z, at, :]
             for p in range(4):
                 sums[p] = sums[p] + frames[z, p, at, :] * field
@@ -314,32 +317,42 @@
         part[pl.ds(pl.multiple_of(8 * n, 8), 8), :] = value
         return carry
 
-    lax.fori_loop(0, 8, atoms, 0)
+    for slot, planes in enumerate(REACHED):
+        lax.fori_loop(2 * slot, 2 * slot + 2, functools.partial(atoms, planes), 0)
 
 
 def spread_back(coeffs, picked, frames, pick_t, out_ref):
-    def atoms(n, carry):
+    def atoms(planes, n, carry):
         value = coeffs[pl.ds(pl.multiple_of(8 * n, 8), 8), :]
         for i in range(8):
             at = pl.ds(pl.multiple_of(64 * n + 8 * i, 8), 8)
             wide = [jnp.broadcast_to(value[i : i + 1, p : p + 1], (8, 128)) for p in range(4)]
             for z in range(8):
+                if z not in planes:
+                    picked[z, at, :] = jnp.zeros((8, 128), F32)
+                    continue
                 total = wide[0] * frames[z, 0, at, :]
                 for p in range(1, 4):
                     total = total + wide[p] * frames[z, p, at, :]
                 picked[z, at, :] = total
         return carry
 
-    lax.fori_loop(0, 8, atoms, 0)
-
-    def planes(n, carry):
+    for slot, planes in enumerate(REACHED):
+        lax.fori_loop(2 * slot, 2 * slot + 2, functools.partial(atoms, planes), 0)
+
+    def rows(n, carry):
         high, low = two_planes(picked, n)
         res = mm(pick_t[...], high) + mm(pick_t[...], low)
         out_ref[2 * n] += res[:, :128]
         out_ref[2 * n + 1] += res[:, 128:]
         return carry
 
-    lax.fori_loop(0, 4, planes, 0)
+    lax.fori_loop(0, 4, rows, 0)
+
+
+def zigzag(k, count):
+    odd = lax.rem(k, 2)
+    return lax.rem(count + (2 * odd - 1) * ((k + 1) // 2), count)
 
 
 class Swap:
@@ -362,7 +375,7 @@
         count = group_size(self.axes)
 
         def step(k, carry):
-            self.remote(lax.rem(self.me + k, count)).start()
+            self.remote(lax.rem(self.me + zigzag(k, count), count)).start()
             return carry
 
         lax.fori_loop(1, count, step, 0)
@@ -488,7 +501,6 @@
 
 def sum_squares(squares, sums, total, send, recv):
     zb = lax.axis_index("zb")
-    eight = pl.ds(0, 8)
 
     def flow(way, half, step):
         turn = 1 if way == 0 else 7
@@ -498,9 +510,9 @@
 
     def own(way, half, away):
         chunk = lax.rem(zb + (16 - away if way == 0 else away), 8)
-        return way, pl.ds(pl.multiple_of(chunk * 16 + half * 8, 8), 8)
-
-    flows = [(way, half) for half in range(2) for way in range(2)]
+        return way, pl.ds(pl.multiple_of(chunk * 16 + half * 4, 4), 4)
+
+    flows = [(way, half) for half in range(4) for way in range(2)]
     for way, half in flows:
         place, dst, one, two = flow(way, half, 0)
         copy_to(squares.at[own(way, half, 1)], dst, one, two, place).start()
@@ -518,7 +530,7 @@
     for way, half in flows:
         place, dst, one, two = flow(way, half, 6)
         copy_to(dst, dst, one, two, place).wait_recv()
-        total[way, 8 * half : 8 * half + 8] = (sums[way, half, 6] + squares[own(way, half, 0)]) * 0.125
+        total[way, 4 * half : 4 * half + 4] = (sums[way, half, 6] + squares[own(way, half, 0)]) * 0.125
 
     wait_all(sums, send)
 
@@ -581,7 +593,7 @@
     )
 
     def to_block(k, carry):
-        there = lax.rem(zb + k, 8)
+        there = lax.rem(zb + zigzag(k, 8), 8)
         for n in range(4):
             line.start_one(4 * there + n)
         return carry
@@ -594,7 +606,7 @@
     out = planes_swap(v, planes.at[0], zsend.at[0], zrecv.at[0])
 
     def arrive(k, carry):
-        there = lax.rem(zb - k + 8, 8)
+        there = lax.rem(zb + 8 - zigzag(k, 8), 8)
         for n in range(4):
             wait_all(line.target(4 * there + n), lrecv.at[4 * there + n])
             if n % 2 == 1:
@@ -749,12 +761,12 @@
             pltpu.VMEM((2, 64, 128), F32),
             pltpu.VMEM((2, 6, 32, 128), F32),
             pltpu.VMEM((64, 128), F32),
-            pltpu.VMEM((2, 2, 7, 8, 8, 128), F32),
+            pltpu.VMEM((2, 4, 7, 4, 8, 128), F32),
             pltpu.VMEM((2, 16, 8, 128), F32),
             pltpu.VMEM((2, 4, 16, N), F32),
             dma(4), dma(4), dma(1), dma(1), dma(1), dma(32), dma(1), dma(1), dma(1), dma(2, 8),
             dma(2), dma(2), dma(2), dma(2), dma(2), dma(2), dma(2), dma(2),
-            dma(1), dma(2, 2, 7), dma(2), dma(2),
+            dma(1), dma(2, 4, 7), dma(2), dma(2),
         ],
         compiler_params=pltpu.CompilerParams(
             collective_id=1, has_side_effects=True, vmem_limit_bytes=62 * 1024 * 1024

time: 234 us -> 231 us (0.987)
  Pallas kernels: 231 us -> 228 us
    pallas_call x1, Pallas kernels: 231 us -> 228 us  [run(): pl.pallas_call(program, out_shape=jax.ShapeDtypeStruct((4, N, N), F32), i...]
where the time goes in v5:
time: 231 us
  Pallas kernels  228 us (99%)
    pallas_call x1, Pallas kernels, run(): pl.pallas_call(program, out_shape=jax.ShapeDtypeStruct((4, N, N), F32), i...  228 us

profile of v5, /device:TPU:1, one launch (start us, length us, event | category | flops | bytes accessed | tf_op | source)
XLA Modules:
  0.0 230.6 jit_solution(651304041814178289)
XLA Ops:
  0.0 228.3 %shard_map.91 = f32[4,256,256]{2,1,0:T(8,128)} custom-call(f32[3]{0:T(128)} %cheb_ref.1, f32[4]{0:T(128)} %kb_ref.1, f32[4,256,256]{2,1,0:T(8,128)} %bitcast.2, f32[4,256,256]{2,1,0:T(8,128)} %pot_ref.1, s32[16,2,128]{2,1,0:T(2,128)} %cells_ref.1, f32[64,128]{1,0:T(8,128)} %bitcast.3, bf16[256,768]{1,0:T(8,128)(2,1)} %constant.6.clone.kl_ref, ...), custom_call_target="tpu_custom_call" | custom-call | tf_op jit(solution)/shard_map/pallas_call | solution.py:739
  228.4 2.3 copy.11
